TPU v7x, 256 devices: a whole 4x4x8 slice. The times are simulated.
256 devices in a mesh: wide: 32 (over y, z), narrow: 8 (over x, core).
Axes of the slice: x: 4, y: 4, z: 8, core: 2. Of those that a mesh axis runs over, the one named last changes fastest.
Arguments:
- obs_blocks: bfloat16 [32, 128, 512, 512], P('wide', None, 'narrow'), may hold values from -6 to 6
- obs_row: int32 [32, 128], P('wide'), may hold values from 0 to 7, never falling along the last dimension, each value on 1 to 32 neighbouring positions
- obs_col: int32 [32, 128], P('wide'), may hold values from 0 to 255
- factors: bfloat16 [256, 512, 256], P('wide', 'narrow'), may hold values from -0.25 to 0.25
Outputs:
- agent_factors: float32 [256, 512, 256], P(('wide', 'narrow'))
Inputs may be any that keep to these rules, and one draw needn't show every extreme that they name: `obs_row`: within each group the rows never fall along the slots; every row 0 to 7 has 1 to 32 slots, and some row exactly 32. `obs_col`: any opponent block, repeats allowed.
All inputs are finite; a program needn't handle non-finite values.
Results may differ from a plain program's by a relative error of at most 0.0003.
Values may be sent and summed in bfloat16 or wider, within the bound.
A program may use at most 128 MiB of HBM per device.

v0:
```python
import jax
import jax.numpy as jnp
from jax import lax
from jax.sharding import PartitionSpec as P

RW = 8
MOST = 32


LAMBDA_REG = 1.0


def solve_rows(rhs, gram):
    chol = jnp.linalg.cholesky(gram)
    forward = lax.linalg.triangular_solve(chol, rhs, left_side=False, lower=True, transpose_a=True)
    return lax.linalg.triangular_solve(
        chol, forward, left_side=False, lower=True, transpose_a=False
    )


def body(obs_blocks, obs_row, obs_col, factors):
    blocks = obs_blocks[0]
    rows = obs_row[0]
    cols = obs_col[0]
    slots, part, width = blocks.shape
    rank = factors.shape[2]
    everything = lax.all_gather(factors, "wide", axis=0, tiled=True)
    selected = everything[cols]
    window = MOST
    row_ids = jnp.arange(RW, dtype=jnp.int32)
    firsts = jnp.sum((rows[None, :] < row_ids[:, None]).astype(jnp.int32), axis=1)
    firsts = jnp.minimum(firsts, slots - window)

    def one_row(items):
        row_id, first = items
        block_win = lax.dynamic_slice_in_dim(blocks, first, window, 0)
        chosen_win = lax.dynamic_slice_in_dim(selected, first, window, 0)
        rows_win = lax.dynamic_slice_in_dim(rows, first, window, 0)
        keep = (rows_win == row_id).astype(jnp.bfloat16)
        masked = chosen_win * keep[:, None, None]
        rhs_row = jnp.einsum("kba,kbr->ar", block_win, masked, preferred_element_type=jnp.float32)
        gram_row = jnp.einsum("kbr,kbs->rs", masked, masked, preferred_element_type=jnp.float32)
        return (rhs_row, gram_row)

    rhs_part, gram_part = lax.map(one_row, (row_ids, firsts))
    identity = jnp.eye(rank, dtype=jnp.float32)[None]
    rhs_total = lax.psum_scatter(rhs_part, "narrow", scatter_dimension=0, tiled=True)
    gram_total = lax.psum_scatter(gram_part, "narrow", scatter_dimension=0, tiled=True)
    solved = solve_rows(rhs_total, gram_total + LAMBDA_REG * identity)
    return solved


def solution(mesh):
    placed = (
        P("wide", None, "narrow", None),
        P("wide", None),
        P("wide", None),
        P("wide", "narrow", None),
    )
    return jax.shard_map(
        body,
        mesh=mesh,
        in_specs=placed,
        out_specs=P(("wide", "narrow"), None, None),
        check_vma=False,
    )
```

profile of v0, /device:TPU:1, one launch (start us, length us, event | category | flops | bytes accessed | tf_op | source)
XLA Modules:
  0.0 308.2 jit_solution(17146130373558633183)
XLA Ops:
  6.5 0.7 all-gather.2.cloned.1.call-update
  7.3 0.8 convert_reduce_fusion
  8.1 0.7 fusion.22
  8.8 103.1 %all-gather.2.cloned.1.call-done = bf16[256,64,256]{2,1,0:T(8,128)(2,1)} async-done(((bf16[8,64,256]{2,1,0:T(8,128)(2,1)}), bf16[256,64,256]{2,1,0:T(8,128)(2,1)}) %all-gather.2.cloned.1.call-update) | async-done | bytes 8388624 | tf_op jit(solution)/shard_map/all_gather | solution.py:27
  111.9 6.2 %gather_fusion = bf16[128,64,256]{2,1,0:T(8,128)(2,1)} fusion(bf16[256,64,256]{2,1,0:T(8,128)(2,1)} %all-gather.2.cloned.1.call-done, s32[1024]{0:T(1024)S(1)} %pad_clamp_fusion), kind=kCustom, calls=%fused_computation | custom fusion | bytes 8389120 | tf_op jit(solution)/shard_map/gather | solution.py:28
  118.1 84.9 %while.13 = (s32[]{:T(128)}, f32[8,512,256]{2,1,0:T(8,128)}, f32[8,256,256]{1,2,0:T(8,128)}, s32[8]{0:T(128)S(1)}, bf16[128,64,512]{2,1,0:T(8,128)(2,1)}, /*inde...) while((s32[]{:T(128)}, f32[8,512,256]{2,1,0:T(8,128)}, ...), condition=%wide.region_2.3_spmd, body=%wide.region_1.2_spmd.sunk | while | flops 806355008 | bytes 4983283 | solution.py:45
  118.1 0.7 dynamic_slice.36
  120.8 0.7 dynamic_slice.37
  121.5 0.8 compare_convert_fusion.2
  122.2 3.5 %fusion.36 = f32[8,512,256]{2,1,0:T(8,128)} fusion(f32[8,512,256]{2,1,0:T(8,128)} %get-tuple-element.182, s32[]{:T(128)} %get-tuple-element.181, bf16[128,64,512]{2,1,0:T(8,128)(2,1)} %get-tuple-element.196, s32[]{:T(128)S(6)} %select_n.26, bf16[128,64,256]{2,1,0:T(8,128)(2,1)} %get-tuple-element.197, bf16[32]{0:T(256)(128)(2,1)S(1)} %compare_convert_fusion.2), kind=kOutput, calls=%fused_computation.4.clone.1 | convolution fusion | flops 537395200 | bytes 3671616 | tf_op jit(solution)/shard_map/while/body/eval_jaxpr/kba,kbr->ar/dot_general | solution.py:41
  125.8 3.1 fusion.37
  128.9 0.7 dynamic_slice.36
  131.6 0.7 dynamic_slice.37
  132.3 0.8 compare_convert_fusion.2
  133.0 3.6 %fusion.36 = f32[8,512,256]{2,1,0:T(8,128)} fusion(f32[8,512,256]{2,1,0:T(8,128)} %get-tuple-element.182, s32[]{:T(128)} %get-tuple-element.181, bf16[128,64,512]{2,1,0:T(8,128)(2,1)} %get-tuple-element.196, s32[]{:T(128)S(6)} %select_n.26, bf16[128,64,256]{2,1,0:T(8,128)(2,1)} %get-tuple-element.197, bf16[32]{0:T(256)(128)(2,1)S(1)} %compare_convert_fusion.2), kind=kOutput, calls=%fused_computation.4.clone.1 | convolution fusion | flops 537395200 | bytes 3671616 | tf_op jit(solution)/shard_map/while/body/eval_jaxpr/kba,kbr->ar/dot_general | solution.py:41
  136.6 2.9 fusion.37
  139.5 0.7 dynamic_slice.36
  142.2 0.7 dynamic_slice.37
  142.9 0.8 compare_convert_fusion.2
  143.7 3.5 %fusion.36 = f32[8,512,256]{2,1,0:T(8,128)} fusion(f32[8,512,256]{2,1,0:T(8,128)} %get-tuple-element.182, s32[]{:T(128)} %get-tuple-element.181, bf16[128,64,512]{2,1,0:T(8,128)(2,1)} %get-tuple-element.196, s32[]{:T(128)S(6)} %select_n.26, bf16[128,64,256]{2,1,0:T(8,128)(2,1)} %get-tuple-element.197, bf16[32]{0:T(256)(128)(2,1)S(1)} %compare_convert_fusion.2), kind=kOutput, calls=%fused_computation.4.clone.1 | convolution fusion | flops 537395200 | bytes 3671616 | tf_op jit(solution)/shard_map/while/body/eval_jaxpr/kba,kbr->ar/dot_general | solution.py:41
  147.1 2.9 fusion.37
  150.0 0.7 dynamic_slice.36
  152.8 0.7 dynamic_slice.37
  153.4 0.8 compare_convert_fusion.2
  154.2 3.5 %fusion.36 = f32[8,512,256]{2,1,0:T(8,128)} fusion(f32[8,512,256]{2,1,0:T(8,128)} %get-tuple-element.182, s32[]{:T(128)} %get-tuple-element.181, bf16[128,64,512]{2,1,0:T(8,128)(2,1)} %get-tuple-element.196, s32[]{:T(128)S(6)} %select_n.26, bf16[128,64,256]{2,1,0:T(8,128)(2,1)} %get-tuple-element.197, bf16[32]{0:T(256)(128)(2,1)S(1)} %compare_convert_fusion.2), kind=kOutput, calls=%fused_computation.4.clone.1 | convolution fusion | flops 537395200 | bytes 3671616 | tf_op jit(solution)/shard_map/while/body/eval_jaxpr/kba,kbr->ar/dot_general | solution.py:41
  157.7 2.9 fusion.37
  160.6 0.7 dynamic_slice.36
  163.4 0.7 dynamic_slice.37
  164.0 0.8 compare_convert_fusion.2
  164.8 3.5 %fusion.36 = f32[8,512,256]{2,1,0:T(8,128)} fusion(f32[8,512,256]{2,1,0:T(8,128)} %get-tuple-element.182, s32[]{:T(128)} %get-tuple-element.181, bf16[128,64,512]{2,1,0:T(8,128)(2,1)} %get-tuple-element.196, s32[]{:T(128)S(6)} %select_n.26, bf16[128,64,256]{2,1,0:T(8,128)(2,1)} %get-tuple-element.197, bf16[32]{0:T(256)(128)(2,1)S(1)} %compare_convert_fusion.2), kind=kOutput, calls=%fused_computation.4.clone.1 | convolution fusion | flops 537395200 | bytes 3671616 | tf_op jit(solution)/shard_map/while/body/eval_jaxpr/kba,kbr->ar/dot_general | solution.py:41
  168.3 2.9 fusion.37
  171.3 0.7 dynamic_slice.36
  174.0 0.7 dynamic_slice.37
  174.7 0.8 compare_convert_fusion.2
  175.4 3.5 %fusion.36 = f32[8,512,256]{2,1,0:T(8,128)} fusion(f32[8,512,256]{2,1,0:T(8,128)} %get-tuple-element.182, s32[]{:T(128)} %get-tuple-element.181, bf16[128,64,512]{2,1,0:T(8,128)(2,1)} %get-tuple-element.196, s32[]{:T(128)S(6)} %select_n.26, bf16[128,64,256]{2,1,0:T(8,128)(2,1)} %get-tuple-element.197, bf16[32]{0:T(256)(128)(2,1)S(1)} %compare_convert_fusion.2), kind=kOutput, calls=%fused_computation.4.clone.1 | convolution fusion | flops 537395200 | bytes 3671616 | tf_op jit(solution)/shard_map/while/body/eval_jaxpr/kba,kbr->ar/dot_general | solution.py:41
  178.9 2.9 fusion.37
  181.9 0.7 dynamic_slice.36
  184.6 0.7 dynamic_slice.37
  185.3 0.8 compare_convert_fusion.2
  186.0 3.5 %fusion.36 = f32[8,512,256]{2,1,0:T(8,128)} fusion(f32[8,512,256]{2,1,0:T(8,128)} %get-tuple-element.182, s32[]{:T(128)} %get-tuple-element.181, bf16[128,64,512]{2,1,0:T(8,128)(2,1)} %get-tuple-element.196, s32[]{:T(128)S(6)} %select_n.26, bf16[128,64,256]{2,1,0:T(8,128)(2,1)} %get-tuple-element.197, bf16[32]{0:T(256)(128)(2,1)S(1)} %compare_convert_fusion.2), kind=kOutput, calls=%fused_computation.4.clone.1 | convolution fusion | flops 537395200 | bytes 3671616 | tf_op jit(solution)/shard_map/while/body/eval_jaxpr/kba,kbr->ar/dot_general | solution.py:41
  189.5 2.9 fusion.37
  192.4 0.7 dynamic_slice.36
  195.2 0.7 dynamic_slice.37
  195.8 0.8 compare_convert_fusion.2
  196.6 3.5 %fusion.36 = f32[8,512,256]{2,1,0:T(8,128)} fusion(f32[8,512,256]{2,1,0:T(8,128)} %get-tuple-element.182, s32[]{:T(128)} %get-tuple-element.181, bf16[128,64,512]{2,1,0:T(8,128)(2,1)} %get-tuple-element.196, s32[]{:T(128)S(6)} %select_n.26, bf16[128,64,256]{2,1,0:T(8,128)(2,1)} %get-tuple-element.197, bf16[32]{0:T(256)(128)(2,1)S(1)} %compare_convert_fusion.2), kind=kOutput, calls=%fused_computation.4.clone.1 | convolution fusion | flops 537395200 | bytes 3671616 | tf_op jit(solution)/shard_map/while/body/eval_jaxpr/kba,kbr->ar/dot_general | solution.py:41
  200.1 2.9 fusion.37
  203.1 0.7 reduce-scatter.3.cloned.1.call-update
  203.8 30.5 %reduce-scatter.5.cloned.1.call-done = f32[1,256,256]{1,2,0:T(8,128)} async-done(((f32[8,256,256]{1,2,0:T(8,128)}), f32[1,256,256]{1,2,0:T(8,128)}) %reduce-scatter.5.cloned.1.call-update) | async-done | bytes 262160 | tf_op jit(solution)/shard_map/reduce_scatter | solution.py:48
  234.3 1.0 convert_add_fusion
  235.4 1.0 fusion.17
  236.4 11.7 %custom-call.18 = f32[1,128,128]{2,1,0:T(8,128)S(1)} custom-call(f32[1,128,128]{2,1,0:T(8,128)S(1)} %cholesky.117), custom_call_target="Cholesky" | custom-call | tf_op jit(solution)/shard_map/jit(cholesky)/cholesky | solution.py:14
  248.1 9.8 %custom-call.19 = f32[1,1,128,128]{2,3,1,0:T(8,128)S(1)} custom-call(f32[1,1,128,128]{3,2,1,0:T(8,128)S(1)} %get-tuple-element.87), custom_call_target="InvertDiagBlocksLowerTriangular" | custom-call | tf_op jit(solution)/shard_map/jit(cholesky)/cholesky | solution.py:14
  258.5 11.7 %custom-call.20 = f32[1,128,128]{2,1,0:T(8,128)S(1)} custom-call(f32[1,128,128]{2,1,0:T(8,128)S(1)} %fusion.15), custom_call_target="Cholesky" | custom-call | tf_op jit(solution)/shard_map/jit(cholesky)/cholesky | solution.py:14
  270.2 0.7 compare_reduce_fusion
  272.3 4.2 %while.14 = (s32[]{:T(128)}, f32[1,256,256]{2,1,0:T(8,128)S(1)}, s32[2,2]{1,0:T(2,128)S(1)}, f32[2,1,128,128]{3,2,1,0:T(8,128)S(1)}, s32[]{:T(128)}) while((s32[]{:T(128)}, f32[1,256,256]{2,1,0:T(8,128)S(1)}, s32[2,2]{1,0:T(2,128)S(1)}, f32[2,1,128,128]{3,2,1,0:T(8,128)S(1)}, s32[]{:T(128)}) %tuple.39), condition=%wide.while_cond, body=%wide.while_body.sunk | while | flops 2 | bytes 131181 | solution.py:15
  272.4 0.7 fusion.38
  273.1 1.3 bitcast_dynamic-update-slice_fusion.3
  274.5 0.7 fusion.38
  275.2 1.3 bitcast_dynamic-update-slice_fusion.3
  276.5 19.7 %custom-call.21 = f32[1,2,128,128]{2,3,1,0:T(8,128)S(1)} custom-call(f32[1,2,128,128]{3,2,1,0:T(8,128)S(1)} %bitcast.97), custom_call_target="InvertDiagBlocksLowerTriangular" | custom-call | tf_op jit(solution)/shard_map/triangular_solve | solution.py:15
  296.2 1.3 fusion.16
  297.6 1.3 fusion.14
  299.7 0.6 convolution_subtract_fusion
  300.7 1.0 copy.13
  (29 shorter events, 2.1 us)
Async XLA Ops:
  6.5 105.4 %all-gather.2.cloned.1.call-start = ((), (), s32[]{:S(2)}) async-start(), calls=%async_computation.2 | async-start | bytes 8650752 | tf_op jit(solution)/shard_map/all_gather | solution.py:27
  7.3 227.0 %reduce-scatter.5.cloned.1.call-start = ((), (), s32[]{:S(2)}) async-start(), calls=%async_computation.4 | async-start | bytes 2359296 | tf_op jit(solution)/shard_map/reduce_scatter | solution.py:48
  8.8 109.3 %copy-start = (s32[1,128]{1,0:T(1,128)S(1)}, s32[1,128]{1,0:T(1,128)}, u32[]{:S(2)}) copy-start(s32[1,128]{1,0:T(1,128)} %param.7) | copy-start | bytes 1540
  203.0 93.2 %reduce-scatter.3.cloned.1.call-start = ((), (), s32[]{:S(2)}) async-start(), calls=%async_computation.3 | async-start | bytes 4718592 | tf_op jit(solution)/shard_map/reduce_scatter | solution.py:47
Sparse Core Ops, SparseCore 0:
  10.0 101.9 all-gather.1
  203.2 31.0 reduce-scatter.4
  236.8 39.2 reduce-scatter.2
where the time goes:
time: 311 us; the launch traced here: 308 us
  waiting for transfers between devices  135 us (43%)
  other arithmetic  63.3 us (20%)
  matrix products  56.4 us (18%)
  local copies, waits for them, and re-layouts  22.1 us (7%)
  loops' own time  16.8 us (5%)
  between operations  14.5 us (5%)
    all_gather x1, waiting for transfers between devices, body(): everything = lax.all_gather(factors, 'wide', axis=0, tiled=True)  103 us
    another operation x6, other arithmetic, solve_rows(): chol = jnp.linalg.cholesky(gram)  34 us
    reduce_scatter x1, waiting for transfers between devices, body(): lax.psum_scatter(gram_part, 'narrow', scatter_dimension=0, tiled=True)  30.5 us
    dot_general x8, matrix products, one_row(): jnp.einsum('kba,kbr->ar', block_win, masked, preferred_element_type=jnp.f...  28.1 us
    dot_general x8, matrix products, one_row(): jnp.einsum('kbr,kbs->rs', masked, masked, preferred_element_type=jnp.floa...  23.4 us
    another operation x3, other arithmetic, solve_rows(): lax.linalg.triangular_solve(chol, rhs, left_side=False, lower=True, trans...  19.7 us
    another operation x1, loops' own time, body(): rhs_part, gram_part = lax.map(one_row, (row_ids, firsts))  16.6 us
    dynamic_slice x16, local copies, waits for them, and re-layouts, body(): rhs_part, gram_part = lax.map(one_row, (row_ids, firsts))  10.6 us
  transfers between devices with their start and end apart: 3, of which 2 were waited for; matrix products, arithmetic and copies ran while one was open for 20% of the time, Pallas kernels for 0%

commit v1 on v0

v1 whole, which is shorter than its diff:
```python
import functools
import heapq

import jax
import jax.numpy as jnp
from jax import lax
from jax.experimental import pallas as pl
from jax.experimental.pallas import tpu as pltpu
from jax.sharding import PartitionSpec as P

RW = 8
MOST = 32
WINDOW = MOST + 2
LAMBDA_REG = 1.0
NY, NZ = 4, 8
MESH = pl.DeviceIdType.MESH

PIECES = (
    ("y", 2, 1, 4, 3, 0, 7),
    ("y", 1, 2, 3, 4, 7, 6),
    ("z", 2, 1, 4, 3, 13, 9),
    ("z", 1, 2, 3, 4, 22, 10),
)
GROUP = 16


def children(piece, dy, dz):
    first, yp, ym, zp, zm = PIECES[piece][:5]
    out = []
    if (first == "y" and dz == 0) or first == "z":
        if 0 <= dy < yp:
            out.append((dy + 1, dz))
        if 0 >= dy > -ym:
            out.append((dy - 1, dz))
    if (first == "z" and dy == 0) or first == "y":
        if 0 <= dz < zp:
            out.append((dy, dz + 1))
        if 0 >= dz > -zm:
            out.append((dy, dz - 1))
    return out


def depth(piece, node):
    kids = children(piece, *node)
    return 1 + max(depth(piece, kid) for kid in kids) if kids else 0


def by_depth(piece, node):
    return sorted(children(piece, *node), key=lambda kid: -depth(piece, kid))


def order_of_arrival(lat=1.0, rate=0.164):
    free, heap, count = {}, [], 0

    def send(now, piece, par, kid):
        link = (kid[0] - par[0], kid[1] - par[1])
        free[link] = max(now, free.get(link, 0.0)) + PIECES[piece][6] * rate
        heapq.heappush(heap, (free[link] + lat, count, piece, kid))

    own = [(piece, kid) for piece in range(len(PIECES)) for kid in children(piece, 0, 0)]
    own.sort(key=lambda edge: -depth(*edge))
    for piece, kid in own:
        send(0.0, piece, (0, 0), kid)
        count += 1
    order = []
    while heap:
        now, _, piece, node = heapq.heappop(heap)
        order.append((piece, node))
        for kid in by_depth(piece, node):
            send(now, piece, node, kid)
            count += 1
    return own, order


def kernel(
    obs_hbm, firsts, rows_s, cols_s, fac_hbm, rhs_ref, gram_ref, fall, obs_v, obs_t, fac_t, win, eye, send_sem, recv_sem, loc_sem
):
    wide = lax.axis_index("wide")
    narrow = lax.axis_index("narrow")
    my_y, my_z = wide // NZ, wide % NZ
    own, order = order_of_arrival()
    number = {edge: at for at, edge in enumerate(order)}
    shard = fac_hbm.shape[0]
    slots = cols_s.shape[0]
    part = obs_hbm.shape[0] // slots
    width = obs_hbm.shape[1]
    rank = fac_hbm.shape[2]
    groups = part // GROUP
    nothing = (fall.shape[0] - groups) // groups
    lanes = 2 * part

    def device(dy, dz):
        return (((my_y + dy + NY) % NY) * NZ + (my_z + dz + NZ) % NZ, narrow)

    fac_copy = pltpu.make_async_copy(fac_hbm, fall.at[pl.ds(wide * shard, shard)], loc_sem.at[0])
    fac_copy.start()
    obs_copy = pltpu.make_async_copy(obs_hbm, obs_v, loc_sem.at[1])
    obs_copy.start()

    barrier = pltpu.get_barrier_semaphore()
    for step in ((1, 0), (-1, 0), (0, 1), (0, -1)):
        pl.semaphore_signal(barrier, inc=1, device_id=device(*step), device_id_type=MESH)
    fac_copy.wait()
    pl.semaphore_wait(barrier, 4)

    def place_of(piece, node):
        source = ((my_y - node[0] + NY) % NY) * NZ + (my_z - node[1] + NZ) % NZ
        return fall.at[pl.ds(source * shard + PIECES[piece][5], PIECES[piece][6])]

    def copy(piece, node, to, step):
        at = number[(piece, to)]
        place = place_of(piece, node)
        return pltpu.make_async_remote_copy(
            src_ref=place,
            dst_ref=place,
            send_sem=send_sem.at[at],
            recv_sem=recv_sem.at[at],
            device_id=device(*step),
            device_id_type=MESH,
        )

    sent = []

    def pass_on(piece, node, kid):
        sent.append(copy(piece, node, kid, (kid[0] - node[0], kid[1] - node[1])))
        sent[-1].start()

    for piece, kid in own:
        pass_on(piece, (0, 0), kid)

    down = lax.broadcasted_iota(jnp.int32, (rank, rank), 0)
    across = lax.broadcasted_iota(jnp.int32, (rank, rank), 1)
    eye[...] = jnp.where(down == across, 1.0, 0.0).astype(jnp.bfloat16)
    for t in range(groups):
        fall[nothing * groups + t] = jnp.zeros((GROUP, rank), jnp.bfloat16)

    def turned(tile):
        flat = lax.dot_general(eye[...], tile, (((1,), (1,)), ((), ())), preferred_element_type=jnp.float32)
        return flat.astype(jnp.bfloat16)

    def block(col):
        return jnp.concatenate([fall[col * groups + t] for t in range(groups)], axis=0)

    obs_copy.wait()
    wide_tiles = width // rank
    tiles = (slots * part // rank) * wide_tiles
    chunks = rank // lanes

    def turn_obs(tile):
        down_at, across_at = tile // wide_tiles, tile % wide_tiles
        flat = turned(obs_v[down_at * rank:(down_at + 1) * rank, across_at * rank:(across_at + 1) * rank])
        for t in range(chunks):
            obs_t[down_at * chunks + t, across_at * rank:(across_at + 1) * rank] = flat[:, t * lanes:(t + 1) * lanes]

    done = 0
    for at, (piece, node) in enumerate(order):
        copy(piece, node, node, (1, 0)).wait_recv()
        for kid in by_depth(piece, node):
            pass_on(piece, node, kid)
        while done < tiles and done * 100 < (at + 1) * tiles:
            turn_obs(done)
            done += 1

    @pl.loop(0, slots * part // rank)
    def turn_factors(step):
        few = rank // part
        flat = turned(jnp.concatenate([block(cols_s[step * few + t]) for t in range(few)], axis=0))
        for t in range(chunks):
            fac_t[step * chunks + t] = flat[:, t * lanes:(t + 1) * lanes]

    def window_of(ref, i):
        first = firsts[i]
        return jnp.concatenate([ref[first + t] for t in range(WINDOW // 2)], axis=1)

    @pl.loop(0, RW)
    def one_gram(i):
        first = firsts[i] * 2
        for t in range(WINDOW):
            col = jnp.where(rows_s[first + t] == i, cols_s[first + t], nothing)
            win[i, t * part:(t + 1) * part, :] = block(col)
        gram_ref[i] = jnp.dot(window_of(fac_t, i), win[i], preferred_element_type=jnp.float32)

    @pl.loop(0, RW)
    def one_rhs(i):
        rhs_ref[i] = jnp.dot(window_of(obs_t, i), win[i], preferred_element_type=jnp.float32)

    for out in sent:
        out.wait_send()


def partials(obs, rows, cols, factors):
    slots, part, width = obs.shape
    rank = factors.shape[-1]
    edges = len(order_of_arrival()[1])
    return pl.pallas_call(
        kernel,
        out_shape=(
            jax.ShapeDtypeStruct((RW, width, rank), jnp.float32),
            jax.ShapeDtypeStruct((RW, rank, rank), jnp.float32),
        ),
        in_specs=[
            pl.BlockSpec(memory_space=pl.ANY),
            pl.BlockSpec(memory_space=pltpu.SMEM),
            pl.BlockSpec(memory_space=pltpu.SMEM),
            pl.BlockSpec(memory_space=pltpu.SMEM),
            pl.BlockSpec(memory_space=pl.ANY),
        ],
        out_specs=(pl.BlockSpec(memory_space=pltpu.VMEM), pl.BlockSpec(memory_space=pltpu.VMEM)),
        scratch_shapes=[
            pltpu.VMEM(((NY * NZ * RW + 1) * part // GROUP, GROUP, rank), jnp.bfloat16),
            pltpu.VMEM((slots * part, width), jnp.bfloat16),
            pltpu.VMEM((slots // 2, width, 2 * part), jnp.bfloat16),
            pltpu.VMEM((slots // 2, rank, 2 * part), jnp.bfloat16),
            pltpu.VMEM((RW, WINDOW * part, rank), jnp.bfloat16),
            pltpu.VMEM((rank, rank), jnp.bfloat16),
            pltpu.SemaphoreType.DMA((edges,)),
            pltpu.SemaphoreType.DMA((edges,)),
            pltpu.SemaphoreType.DMA((2,)),
        ],
        compiler_params=pltpu.CompilerParams(collective_id=0, has_side_effects=True, vmem_limit_bytes=60 * 1024 * 1024),
        name="gather_and_multiply",
    )(
        obs.reshape(slots * part, width),
        window_starts(rows),
        rows,
        cols,
        factors.reshape(-1, GROUP, rank),
    )


def window_starts(rows):
    before = jnp.sum((rows[None, :] < jnp.arange(RW, dtype=jnp.int32)[:, None]).astype(jnp.int32), axis=1)
    return jnp.minimum(before // 2, (rows.shape[0] - WINDOW) // 2)


def solve_rows(rhs, gram):
    chol = jnp.linalg.cholesky(gram)
    forward = lax.linalg.triangular_solve(chol, rhs, left_side=False, lower=True, transpose_a=True)
    return lax.linalg.triangular_solve(
        chol, forward, left_side=False, lower=True, transpose_a=False
    )


def body(obs_blocks, obs_row, obs_col, factors):
    rank = factors.shape[2]
    rhs_part, gram_part = partials(obs_blocks[0], obs_row[0], obs_col[0], factors)
    identity = jnp.eye(rank, dtype=jnp.float32)[None]
    rhs_total = lax.psum_scatter(rhs_part, "narrow", scatter_dimension=0, tiled=True)
    gram_total = lax.psum_scatter(gram_part, "narrow", scatter_dimension=0, tiled=True)
    return solve_rows(rhs_total, gram_total + LAMBDA_REG * identity)


def solution(mesh):
    placed = (
        P("wide", None, "narrow", None),
        P("wide", None),
        P("wide", None),
        P("wide", "narrow", None),
    )
    return jax.shard_map(
        body,
        mesh=mesh,
        in_specs=placed,
        out_specs=P(("wide", "narrow"), None, None),
        check_vma=False,
    )
```

time: 311 us -> 196 us (0.63)
  waiting for transfers between devices: 135 us -> 33.2 us
  Pallas kernels: 0 us -> 76.2 us
  matrix products: 56.4 us -> 4.85 us
  loops' own time: 16.8 us -> 0.21 us
  local copies, waits for them, and re-layouts: 22.1 us -> 7.98 us
  other arithmetic: 63.3 us -> 57 us
    all_gather x1 -> x0, waiting for transfers between devices: 103 us -> none  [body(): everything = lax.all_gather(factors, 'wide', axis=0, tiled=True)]
    pallas_call x0 -> x1, Pallas kernels: none -> 76.2 us  [partials(): pl.pallas_call(kernel, out_shape=(jax.ShapeDtypeStruct((RW, width, rank),...]
    dot_general x16 -> x0, matrix products: 51.5 us -> none  [the longest x8 28.1 us: one_row(): jnp.einsum('kba,kbr->ar', block_win, masked, preferred_element_type=jnp.f...]
    another operation x1 -> x0, loops' own time: 16.6 us -> none  [body(): rhs_part, gram_part = lax.map(one_row, (row_ids, firsts))]
    dynamic_slice x16 -> x0, local copies, waits for them, and re-layouts: 10.6 us -> none  [body(): rhs_part, gram_part = lax.map(one_row, (row_ids, firsts))]
    gather x1 -> x0, local copies, waits for them, and re-layouts: 6.17 us -> none  [body(): selected = everything[cols]]
    convert_element_type x8 -> x0, other arithmetic: 6.12 us -> none  [one_row(): keep = (rows_win == row_id).astype(jnp.bfloat16)]
  transfers between devices with their start and end apart: 3 -> 2, of which waited for: 2 -> 1; matrix products, arithmetic and copies ran while one was open for 20% -> 31% of each run, Pallas kernels for 0% -> 0%
where the time goes in v1:
time: 196 us; the launch traced here: 194 us
  Pallas kernels  76.2 us (39%)
  other arithmetic  57 us (29%)
  waiting for transfers between devices  33.2 us (17%)
  between operations  14.8 us (8%)
  local copies, waits for them, and re-layouts  7.98 us (4%)
  matrix products  4.85 us (2%)
    pallas_call x1, Pallas kernels, partials(): pl.pallas_call(kernel, out_shape=(jax.ShapeDtypeStruct((RW, width, rank),...  76.2 us
    another operation x6, other arithmetic, solve_rows(): chol = jnp.linalg.cholesky(gram)  34 us
    reduce_scatter x1, waiting for transfers between devices, body(): lax.psum_scatter(gram_part, 'narrow', scatter_dimension=0, tiled=True)  32.6 us
    another operation x3, other arithmetic, solve_rows(): lax.linalg.triangular_solve(chol, rhs, left_side=False, lower=True, trans...  19.7 us
  transfers between devices with their start and end apart: 2, of which 1 were waited for; matrix products, arithmetic and copies ran while one was open for 31% of the time, Pallas kernels for 0%

profile of v1, /device:TPU:1, one launch (start us, length us, event | category | flops | bytes accessed | tf_op | source)
XLA Modules:
  0.0 194.4 jit_solution(3701033339811862006)
XLA Ops:
  6.5 0.0 reduce-scatter.5.cloned.1.call-start
  6.5 0.8 convert_reduce_fusion
  7.3 0.5 fusion.9.firsts
  7.8 76.2 %gather_and_multiply.1 = (f32[8,512,256]{2,1,0:T(8,128)}, f32[8,256,256]{2,1,0:T(8,128)}) custom-call(bf16[8192,512]{1,0:T(8,128)(2,1)} %bitcast.70, s32[8]{0:T(128)} %fusion.9.firsts, s32[128]{0:T(128)} %bitcast.74, s32[128]{0:T(128)} %bitcast.75, bf16[32,16,256]{2,1,0:T(8,128)(2,1)} %bitcast.72), custom_call_target="tpu_custom_call" | custom-call | tf_op jit(solution)/shard_map/gather_and_multiply/pallas_call | solution.py:195
  84.1 2.9 %copy.8 = f32[8,256,256]{1,2,0:T(8,128)} copy(f32[8,256,256]{2,1,0:T(8,128)} %get-tuple-element.8) | data formatting | bytes 4194304 | tf_op jit(solution)/shard_map/gather_and_multiply/pallas_call | solution.py:195
  87.0 0.0 reduce-scatter.5.cloned.1.call-update
  87.0 0.2 reduce-scatter.3.cloned.1.call-start
  87.2 0.5 reduce-scatter.3.cloned.1.call-update
  87.8 32.6 %reduce-scatter.5.cloned.1.call-done = f32[1,256,256]{1,2,0:T(8,128)} async-done(((f32[8,256,256]{1,2,0:T(8,128)}), f32[1,256,256]{1,2,0:T(8,128)}) %reduce-scatter.5.cloned.1.call-update) | async-done | bytes 262160 | tf_op jit(solution)/shard_map/reduce_scatter | solution.py:249
  120.4 1.0 convert_add_fusion
  121.4 0.1 copy.9
  121.5 1.0 fusion.4
  122.5 11.7 %custom-call.18 = f32[1,128,128]{2,1,0:T(8,128)S(1)} custom-call(f32[1,128,128]{2,1,0:T(8,128)S(1)} %cholesky.117), custom_call_target="Cholesky" | custom-call | tf_op jit(solution)/shard_map/jit(cholesky)/cholesky | solution.py:237
  134.3 9.8 %custom-call.19 = f32[1,1,128,128]{2,3,1,0:T(8,128)S(1)} custom-call(f32[1,1,128,128]{3,2,1,0:T(8,128)S(1)} %get-tuple-element.30), custom_call_target="InvertDiagBlocksLowerTriangular" | custom-call | tf_op jit(solution)/shard_map/jit(cholesky)/cholesky | solution.py:237
  144.1 0.2 bitcast_dynamic-update-slice_fusion.1
  144.3 0.3 fusion.2
  144.6 11.7 %custom-call.20 = f32[1,128,128]{2,1,0:T(8,128)S(1)} custom-call(f32[1,128,128]{2,1,0:T(8,128)S(1)} %fusion.2), custom_call_target="Cholesky" | custom-call | tf_op jit(solution)/shard_map/jit(cholesky)/cholesky | solution.py:237
  156.4 0.7 compare_reduce_fusion
  158.3 0.1 triangular_solve.72
  158.4 4.0 %while.1 = (s32[]{:T(128)}, f32[1,256,256]{2,1,0:T(8,128)S(1)}, s32[2,2]{1,0:T(2,128)S(1)}, f32[2,1,128,128]{3,2,1,0:T(8,128)S(1)}, s32[]{:T(128)}) while((s32[]{:T(128)}, f32[1,256,256]{2,1,0:T(8,128)S(1)}, s32[2,2]{1,0:T(2,128)S(1)}, f32[2,1,128,128]{3,2,1,0:T(8,128)S(1)}, s32[]{:T(128)}) %tuple.23), condition=%wide.while_cond, body=%wide.while_body.sunk | while | flops 2 | bytes 131189 | solution.py:238
  158.6 0.6 fusion.19
  159.2 1.3 bitcast_dynamic-update-slice_fusion.3
  160.5 0.6 fusion.19
  161.1 1.3 bitcast_dynamic-update-slice_fusion.3
  162.4 19.7 %custom-call.21 = f32[1,2,128,128]{2,3,1,0:T(8,128)S(1)} custom-call(f32[1,2,128,128]{3,2,1,0:T(8,128)S(1)} %bitcast.76), custom_call_target="InvertDiagBlocksLowerTriangular" | custom-call | tf_op jit(solution)/shard_map/triangular_solve | solution.py:238
  182.1 0.0 reduce-scatter.3.cloned.1.call-done
  182.1 1.3 fusion.3
  183.5 1.3 fusion.1
  184.8 0.4 fusion.8
  185.2 0.4 fusion.7
  185.6 0.6 convolution_subtract_fusion
  186.2 0.4 convolution_bitcast_fusion
  186.6 1.0 copy.10
  (10 shorter events, 0.2 us)
Async XLA Ops:
  6.5 113.9 %reduce-scatter.5.cloned.1.call-start = ((), (), s32[]{:S(2)}) async-start(), calls=%async_computation.3 | async-start | bytes 2359296 | tf_op jit(solution)/shard_map/reduce_scatter | solution.py:249
  87.0 95.1 %reduce-scatter.3.cloned.1.call-start = ((), (), s32[]{:S(2)}) async-start(), calls=%async_computation.2 | async-start | bytes 4718592 | tf_op jit(solution)/shard_map/reduce_scatter | solution.py:248
Sparse Core Ops, SparseCore 0:
  87.1 33.2 reduce-scatter.4
  123.0 39.3 reduce-scatter.2

commit v2 on v1

--- a/solution.py
+++ b/solution.py
@@ -12,7 +12,7 @@
 MOST = 32
 WINDOW = MOST + 2
 LAMBDA_REG = 1.0
-NY, NZ = 4, 8
+NX, NY, NZ = 4, 4, 8
 MESH = pl.DeviceIdType.MESH
 
 PIECES = (
@@ -22,6 +22,7 @@
     ("z", 1, 2, 3, 4, 22, 10),
 )
 GROUP = 16
+PANEL = 32
 
 
 def children(piece, dy, dz):
@@ -72,8 +73,114 @@
     return own, order
 
 
+class RowSum:
+    def __init__(self, rows, pair, ring, send_sem, recv_sem, base, my_x, my_core, beside):
+        self.rows, self.pair, self.ring = rows, pair, ring
+        self.send_sem, self.recv_sem, self.base = send_sem, recv_sem, base
+        self.my_x, self.my_core, self.beside = my_x, my_core, beside
+        self.half = rows.shape[1] // 2
+        self.sent = []
+
+    def chip(self, ahead):
+        return (self.my_x + ahead + NX) % NX
+
+    def row(self, ahead, other):
+        return self.chip(ahead) * 2 + (1 - self.my_core if other else self.my_core)
+
+    def near(self, ahead, q):
+        return pltpu.make_async_remote_copy(
+            src_ref=self.rows.at[self.row(ahead, True)],
+            dst_ref=self.pair.at[self.chip(ahead)],
+            send_sem=self.send_sem.at[self.base + q],
+            recv_sem=self.recv_sem.at[self.base + q],
+            device_id=self.beside(0, 1),
+            device_id_type=MESH,
+        )
+
+    def hop(self, slot, ahead, upper, step):
+        at = self.base + 4 + slot
+        return pltpu.make_async_remote_copy(
+            src_ref=self.rows.at[self.row(ahead, False), pl.ds(self.half if upper else 0, self.half)],
+            dst_ref=self.ring.at[slot],
+            send_sem=self.send_sem.at[at],
+            recv_sem=self.recv_sem.at[at],
+            device_id=self.beside(step, 0),
+            device_id_type=MESH,
+        )
+
+    def start(self, *what):
+        self.sent.append(self.hop(*what))
+        self.sent[-1].start()
+
+    def arrived(self, slot):
+        self.hop(slot, 1, False, 1).wait_recv()
+
+    def fold(self, q):
+        ahead = (2 - q + NX) % NX
+        self.near(ahead, q).wait_recv()
+        mine = self.row(ahead, False)
+        self.rows[mine] = self.rows[mine] + self.pair[self.chip(ahead)]
+        if ahead == 2:
+            self.start(0, 2, False, 1)
+            self.start(1, 2, True, -1)
+        elif ahead == 1:
+            self.start(2, 1, True, 1)
+        elif ahead == 3:
+            self.start(3, 3, False, -1)
+
+    def forward(self):
+        half = self.half
+        self.arrived(0)
+        up = self.row(1, False)
+        self.rows[up, 0:half] = self.rows[up, 0:half] + self.ring[0]
+        self.start(4, 1, False, 1)
+        self.arrived(1)
+        back = self.row(3, False)
+        self.rows[back, half:2 * half] = self.rows[back, half:2 * half] + self.ring[1]
+        self.start(5, 3, True, -1)
+
+    def total(self):
+        for slot in (2, 3, 4, 5):
+            self.arrived(slot)
+        mine, half = self.row(0, False), self.half
+        low = self.rows[mine, 0:half] + self.ring[4] + self.ring[3]
+        high = self.rows[mine, half:2 * half] + self.ring[5] + self.ring[2]
+        return low, high
+
+    def finish(self):
+        for q in range(NX):
+            self.near((2 - q + NX) % NX, q).wait_send()
+        for out in self.sent:
+            out.wait_send()
+
+
+def small_inverse(block):
+    size = block.shape[0]
+    down = lax.broadcasted_iota(jnp.int32, (size, size), 0)
+    across = lax.broadcasted_iota(jnp.int32, (size, size), 1)
+    for j in range(size):
+        pivot = 1.0 / block[j:j + 1, j:j + 1]
+        row = jnp.where(across[j:j + 1] == j, pivot, block[j:j + 1] * pivot)
+        col = block[:, j:j + 1]
+        block = jnp.where(down == j, row, jnp.where(across == j, 0.0, block) - col * row)
+    return block
+
+
+def eliminate(inv, low, high):
+    pivot = small_inverse(inv[low:high, low:high])
+    rows = jnp.dot(pivot, inv[low:high, :], precision=lax.Precision.HIGHEST, preferred_element_type=jnp.float32)
+    cols = inv[:, low:high]
+    change = jnp.dot(cols, rows, precision=lax.Precision.HIGHEST, preferred_element_type=jnp.float32)
+    side = jnp.dot(cols, pivot, precision=lax.Precision.HIGHEST, preferred_element_type=jnp.float32)
+    inv[...] = inv[...] - change
+    inv[:, low:high] = -side
+    inv[low:high, :] = rows
+    inv[low:high, low:high] = pivot
+
+
 def kernel(
-    obs_hbm, firsts, rows_s, cols_s, fac_hbm, rhs_ref, gram_ref, fall, obs_v, obs_t, fac_t, win, eye, send_sem, recv_sem, loc_sem
+    obs_hbm, firsts, rows_s, cols_s, fac_hbm, out_ref, fall, obs_v, obs_t, fac_t, win, eye,
+    gram, gram_near, gram_ring, rhs, rhs_near, rhs_ring, inv, send_sem, recv_sem, loc_sem, sum_send, sum_recv
 ):
     wide = lax.axis_index("wide")
     narrow = lax.axis_index("narrow")
@@ -92,16 +199,24 @@
     def device(dy, dz):
         return (((my_y + dy + NY) % NY) * NZ + (my_z + dz + NZ) % NZ, narrow)
 
+    my_x, my_core = narrow // 2, narrow % 2
+
+    def beside(dx, other):
+        core = 1 - my_core if other else my_core
+        return (wide, (my_x + dx + NX) % NX * 2 + core)
+
     fac_copy = pltpu.make_async_copy(fac_hbm, fall.at[pl.ds(wide * shard, shard)], loc_sem.at[0])
     fac_copy.start()
     obs_copy = pltpu.make_async_copy(obs_hbm, obs_v, loc_sem.at[1])
     obs_copy.start()
 
     barrier = pltpu.get_barrier_semaphore()
-    for step in ((1, 0), (-1, 0), (0, 1), (0, -1)):
-        pl.semaphore_signal(barrier, inc=1, device_id=device(*step), device_id_type=MESH)
+    partners = [device(*step) for step in ((1, 0), (-1, 0), (0, 1), (0, -1))]
+    partners += [beside(0, 1), beside(1, 0), beside(-1, 0)]
+    for partner in partners:
+        pl.semaphore_signal(barrier, inc=1, device_id=partner, device_id_type=MESH)
     fac_copy.wait()
-    pl.semaphore_wait(barrier, 4)
+    pl.semaphore_wait(barrier, len(partners))
 
     def place_of(piece, node):
         source = ((my_y - node[0] + NY) % NY) * NZ + (my_z - node[1] + NZ) % NZ
@@ -172,32 +287,76 @@
         first = firsts[i]
         return jnp.concatenate([ref[first + t] for t in range(WINDOW // 2)], axis=1)
 
-    @pl.loop(0, RW)
-    def one_gram(i):
-        first = firsts[i] * 2
+    gram_sum = RowSum(gram, gram_near, gram_ring, sum_send, sum_recv, 0, my_x, my_core, beside)
+    rhs_sum = RowSum(rhs, rhs_near, rhs_ring, sum_send, sum_recv, 10, my_x, my_core, beside)
+    half = rank // 2
+
+    def gram_of(row):
+        first = firsts[row] * 2
         for t in range(WINDOW):
-            col = jnp.where(rows_s[first + t] == i, cols_s[first + t], nothing)
-            win[i, t * part:(t + 1) * part, :] = block(col)
-        gram_ref[i] = jnp.dot(window_of(fac_t, i), win[i], preferred_element_type=jnp.float32)
-
-    @pl.loop(0, RW)
-    def one_rhs(i):
-        rhs_ref[i] = jnp.dot(window_of(obs_t, i), win[i], preferred_element_type=jnp.float32)
-
+            col = jnp.where(rows_s[first + t] == row, cols_s[first + t], nothing)
+            win[row, t * part:(t + 1) * part, :] = block(col)
+        whole = jnp.dot(window_of(fac_t, row), win[row], preferred_element_type=jnp.float32)
+        gram[row, 0:rank, :] = whole[:, :half]
+        gram[row, rank:rank + half, :] = whole[half:, half:]
+
+    def rhs_of(row):
+        rhs[row] = jnp.dot(window_of(obs_t, row), win[row], preferred_element_type=jnp.float32)
+
+    @pl.loop(0, NX)
+    def grams(q):
+        ahead = (2 - q + NX) % NX
+        gram_of(gram_sum.row(ahead, True))
+        gram_sum.near(ahead, q).start()
+        gram_of(gram_sum.row(ahead, False))
+
+    def rhs_pair(q):
+        ahead = (2 - q + NX) % NX
+        rhs_of(rhs_sum.row(ahead, True))
+        rhs_sum.near(ahead, q).start()
+        rhs_of(rhs_sum.row(ahead, False))
+
+    for q in range(NX):
+        gram_sum.fold(q)
+    pl.loop(0, 2)(rhs_pair)
+    gram_sum.forward()
+    rhs_sum.fold(0)
+    rhs_sum.fold(1)
+    pl.loop(2, NX)(rhs_pair)
+    rhs_sum.fold(2)
+    rhs_sum.fold(3)
+
+    low, high = gram_sum.total()
+    packed = jnp.concatenate([low, high], axis=0)
+    same = jnp.where(down == across, LAMBDA_REG, 0.0)
+    inv[:half, :half] = packed[:half] + same[:half, :half]
+    inv[half:, :half] = packed[half:rank]
+    inv[:half, half:] = packed[half:rank].T
+    inv[half:, half:] = packed[rank:] + same[:half, :half]
+
+    panels = rank // PANEL
+    for p in range(panels):
+        if p == panels // 2:
+            rhs_sum.forward()
+        eliminate(inv, p * PANEL, (p + 1) * PANEL)
+
+    low, high = rhs_sum.total()
+    out_ref[0:width // 2] = jnp.dot(low, inv[...], precision=lax.Precision.HIGHEST, preferred_element_type=jnp.float32)
+    out_ref[width // 2:] = jnp.dot(high, inv[...], precision=lax.Precision.HIGHEST, preferred_element_type=jnp.float32)
+
+    gram_sum.finish()
+    rhs_sum.finish()
     for out in sent:
         out.wait_send()
 
 
-def partials(obs, rows, cols, factors):
+def solved_row(obs, rows, cols, factors):
     slots, part, width = obs.shape
     rank = factors.shape[-1]
     edges = len(order_of_arrival()[1])
     return pl.pallas_call(
         kernel,
-        out_shape=(
-            jax.ShapeDtypeStruct((RW, width, rank), jnp.float32),
-            jax.ShapeDtypeStruct((RW, rank, rank), jnp.float32),
-        ),
+        out_shape=jax.ShapeDtypeStruct((width, rank), jnp.float32),
         in_specs=[
             pl.BlockSpec(memory_space=pl.ANY),
             pl.BlockSpec(memory_space=pltpu.SMEM),
@@ -205,7 +364,7 @@
             pl.BlockSpec(memory_space=pltpu.SMEM),
             pl.BlockSpec(memory_space=pl.ANY),
         ],
-        out_specs=(pl.BlockSpec(memory_space=pltpu.VMEM), pl.BlockSpec(memory_space=pltpu.VMEM)),
+        out_specs=pl.BlockSpec(memory_space=pltpu.VMEM),
         scratch_shapes=[
             pltpu.VMEM(((NY * NZ * RW + 1) * part // GROUP, GROUP, rank), jnp.bfloat16),
             pltpu.VMEM((slots * part, width), jnp.bfloat16),
@@ -213,12 +372,21 @@
             pltpu.VMEM((slots // 2, rank, 2 * part), jnp.bfloat16),
             pltpu.VMEM((RW, WINDOW * part, rank), jnp.bfloat16),
             pltpu.VMEM((rank, rank), jnp.bfloat16),
+            pltpu.VMEM((RW, rank + rank // 2, rank // 2), jnp.float32),
+            pltpu.VMEM((NX, rank + rank // 2, rank // 2), jnp.float32),
+            pltpu.VMEM((6, (rank + rank // 2) // 2, rank // 2), jnp.float32),
+            pltpu.VMEM((RW, width, rank), jnp.float32),
+            pltpu.VMEM((NX, width, rank), jnp.float32),
+            pltpu.VMEM((6, width // 2, rank), jnp.float32),
+            pltpu.VMEM((rank, rank), jnp.float32),
             pltpu.SemaphoreType.DMA((edges,)),
             pltpu.SemaphoreType.DMA((edges,)),
             pltpu.SemaphoreType.DMA((2,)),
+            pltpu.SemaphoreType.DMA((20,)),
+            pltpu.SemaphoreType.DMA((20,)),
         ],
         compiler_params=pltpu.CompilerParams(collective_id=0, has_side_effects=True, vmem_limit_bytes=60 * 1024 * 1024),
-        name="gather_and_multiply",
+        name="solve_rows",
     )(
         obs.reshape(slots * part, width),
         window_starts(rows),
@@ -233,21 +401,8 @@
     return jnp.minimum(before // 2, (rows.shape[0] - WINDOW) // 2)
 
 
-def solve_rows(rhs, gram):
-    chol = jnp.linalg.cholesky(gram)
-    forward = lax.linalg.triangular_solve(chol, rhs, left_side=False, lower=True, transpose_a=True)
-    return lax.linalg.triangular_solve(
-        chol, forward, left_side=False, lower=True, transpose_a=False
-    )
-
-
 def body(obs_blocks, obs_row, obs_col, factors):
-    rank = factors.shape[2]
-    rhs_part, gram_part = partials(obs_blocks[0], obs_row[0], obs_col[0], factors)
-    identity = jnp.eye(rank, dtype=jnp.float32)[None]
-    rhs_total = lax.psum_scatter(rhs_part, "narrow", scatter_dimension=0, tiled=True)
-    gram_total = lax.psum_scatter(gram_part, "narrow", scatter_dimension=0, tiled=True)
-    return solve_rows(rhs_total, gram_total + LAMBDA_REG * identity)
+    return solved_row(obs_blocks[0], obs_row[0], obs_col[0], factors)[None]
 
 
 def solution(mesh):

time: 196 us -> 118 us (0.60)
  other arithmetic: 57 us -> 1.29 us
  Pallas kernels: 76.2 us -> 114 us
  waiting for transfers between devices: 33.2 us -> 0 us
  between operations: 14.8 us -> 0.01 us
  local copies, waits for them, and re-layouts: 7.98 us -> 1.87 us
  matrix products: 4.85 us -> 0 us
    another operation x10 -> x0, other arithmetic: 53.7 us -> none  [the longest x6 34 us: solve_rows(): chol = jnp.linalg.cholesky(gram)]
    pallas_call x1, Pallas kernels: 76.2 us -> 114 us  [solved_row(): pl.pallas_call(kernel, out_shape=jax.ShapeDtypeStruct((width, rank), jnp....]
    reduce_scatter x2 -> x0, waiting for transfers between devices: 32.7 us -> none  [the longest x1 32.6 us: body(): lax.psum_scatter(gram_part, 'narrow', scatter_dimension=0, tiled=True)]
    another operation x10 -> x0, local copies, waits for them, and re-layouts: 4.92 us -> none
    another operation x8 -> x0, matrix products: 4.85 us -> none  [the longest x3 3.01 us: solve_rows(): lax.linalg.triangular_solve(chol, rhs, left_side=False, lower=True, trans...]
    pallas_call x1 -> x0, local copies, waits for them, and re-layouts: 2.93 us -> none  [partials(): pl.pallas_call(kernel, out_shape=(jax.ShapeDtypeStruct((RW, width, rank),...]
  transfers between devices with their start and end apart: 2 -> 0, of which waited for: 1 -> 0; matrix products, arithmetic and copies ran while one was open for 31% -> 0% of each run, Pallas kernels for 0% -> 0%
where the time goes in v2:
time: 118 us; the launch traced here: 117 us
  Pallas kernels  114 us (97%)
  local copies, waits for them, and re-layouts  1.87 us (2%)
  other arithmetic  1.29 us (1%)
    pallas_call x1, Pallas kernels, solved_row(): pl.pallas_call(kernel, out_shape=jax.ShapeDtypeStruct((width, rank), jnp....  114 us

profile of v2, /device:TPU:1, one launch (start us, length us, event | category | flops | bytes accessed | tf_op | source)
XLA Modules:
  0.0 117.4 jit_solution(17349603721127271294)
XLA Ops:
  0.0 0.8 convert_reduce_fusion
  0.8 0.5 fusion.firsts
  1.3 114.2 %solve_rows.1 = f32[512,256]{1,0:T(8,128)} custom-call(bf16[8192,512]{1,0:T(8,128)(2,1)} %bitcast.5, s32[8]{0:T(128)} %fusion.firsts, s32[128]{0:T(128)} %bitcast.9, s32[128]{0:T(128)} %bitcast.10, bf16[32,16,256]{2,1,0:T(8,128)(2,1)} %bitcast.7), custom_call_target="tpu_custom_call" | custom-call | tf_op jit(solution)/shard_map/solve_rows/pallas_call | solution.py:357
  115.5 1.9 %copy.6 = f32[1,512,256]{2,1,0:T(8,128)} copy(f32[1,512,256]{2,1,0:T(8,128)} %bitcast.6) | data formatting | bytes 1048576

commit v3 on v2

--- a/solution.py
+++ b/solution.py
@@ -22,7 +22,7 @@
     ("z", 1, 2, 3, 4, 22, 10),
 )
 GROUP = 16
-PANEL = 32
+PANEL = 64
 
 
 def children(piece, dy, dz):
@@ -154,33 +154,74 @@
             out.wait_send()
 
 
+def inverse_2x2(a, b, c):
+    scale = 1.0 / (a * c - b * b)
+    return c * scale, -b * scale, a * scale
+
+
+def inverse_4x4(m):
+    a, b, c = inverse_2x2(m[0][0], m[0][1], m[1][1])
+    top = [[a * m[0][k] + b * m[1][k] for k in (2, 3)], [b * m[0][k] + c * m[1][k] for k in (2, 3)]]
+
+    def rest(k, l):
+        return m[k][l] - (m[0][k] * top[0][l - 2] + m[1][k] * top[1][l - 2])
+
+    p, q, r = inverse_2x2(rest(2, 2), rest(2, 3), rest(3, 3))
+    side = [[-(top[k][0] * p + top[k][1] * q), -(top[k][0] * q + top[k][1] * r)] for k in (0, 1)]
+    aa = a - (side[0][0] * top[0][0] + side[0][1] * top[0][1])
+    bb = b - (side[0][0] * top[1][0] + side[0][1] * top[1][1])
+    cc = c - (side[1][0] * top[1][0] + side[1][1] * top[1][1])
+    return [
+        [aa, bb, side[0][0], side[0][1]],
+        [bb, cc, side[1][0], side[1][1]],
+        [side[0][0], side[1][0], p, q],
+        [side[0][1], side[1][1], q, r],
+    ]
+
+
 def small_inverse(block):
     size = block.shape[0]
     down = lax.broadcasted_iota(jnp.int32, (size, size), 0)
     across = lax.broadcasted_iota(jnp.int32, (size, size), 1)
-    for j in range(size):
-        pivot = 1.0 / block[j:j + 1, j:j + 1]
-        row = jnp.where(across[j:j + 1] == j, pivot, block[j:j + 1] * pivot)
-        col = block[:, j:j + 1]
-        block = jnp.where(down == j, row, jnp.where(across == j, 0.0, block) - col * row)
+    lane = across[0:8]
+    for j in range(0, size, 4):
+        cols = [jnp.broadcast_to(block[:, j + k:j + k + 1], (size, size)) for k in range(4)]
+        rows = [jnp.broadcast_to(block[j + k:j + k + 1], (8, size)) for k in range(4)]
+        pivot = [[jnp.broadcast_to(cols[max(k, l)][j + min(k, l):j + min(k, l) + 1], (8, size)) for l in range(4)] for k in range(4)]
+        inverse = inverse_4x4(pivot)
+        rest = jnp.where((across >= j) & (across < j + 4), 0.0, block)
+        done = []
+        for k in range(4):
+            row = (inverse[k][0] * rows[0] + inverse[k][1] * rows[1]) + (inverse[k][2] * rows[2] + inverse[k][3] * rows[3])
+            for l in range(4):
+                row = jnp.where(lane == j + l, inverse[k][l], row)
+            done.append(jnp.concatenate([row] * (size // 8), axis=0))
+        rest = rest - ((cols[0] * done[0] + cols[1] * done[1]) + (cols[2] * done[2] + cols[3] * done[3]))
+        for k in range(4):
+            rest = jnp.where(down == j + k, done[k], rest)
+        block = rest
     return block
+
+
+def exact_dot(x, y):
+    return jnp.dot(x, y, precision=lax.Precision.HIGHEST, preferred_element_type=jnp.float32)
 
 
 def eliminate(inv, low, high):
     pivot = small_inverse(inv[low:high, low:high])
-    rows = jnp.dot(pivot, inv[low:high, :], precision=lax.Precision.HIGHEST, preferred_element_type=jnp.float32)
-    cols = inv[:, low:high]
-    change = jnp.dot(cols, rows, precision=lax.Precision.HIGHEST, preferred_element_type=jnp.float32)
-    side = jnp.dot(cols, pivot, precision=lax.Precision.HIGHEST, preferred_element_type=jnp.float32)
-    inv[...] = inv[...] - change
-    inv[:, low:high] = -side
-    inv[low:high, :] = rows
+    inv[low:high, :] = exact_dot(pivot, inv[low:high, :])
     inv[low:high, low:high] = pivot
+    rows = inv[low:high, :]
+    for part in ((0, low), (high, inv.shape[0])):
+        if part[0] < part[1]:
+            cols = inv[part[0]:part[1], low:high]
+            inv[part[0]:part[1], low:high] = jnp.zeros_like(cols)
+            inv[part[0]:part[1], :] = inv[part[0]:part[1], :] - exact_dot(cols, rows)
 
 
 def kernel(
     obs_hbm, firsts, rows_s, cols_s, fac_hbm, out_ref, fall, obs_v, obs_t, fac_t, win, eye,
-    gram, gram_near, gram_ring, rhs, rhs_near, rhs_ring, inv, send_sem, recv_sem, loc_sem, sum_send, sum_recv
+    gram, gram_near, gram_ring, rhs, rhs_near, rhs_ring, inv, whole_gram, send_sem, recv_sem, loc_sem, sum_send, sum_recv
 ):
     wide = lax.axis_index("wide")
     narrow = lax.axis_index("narrow")
@@ -334,15 +375,17 @@
     inv[:half, half:] = packed[half:rank].T
     inv[half:, half:] = packed[rank:] + same[:half, :half]
 
+    whole_gram[...] = inv[...]
     panels = rank // PANEL
     for p in range(panels):
         if p == panels // 2:
             rhs_sum.forward()
         eliminate(inv, p * PANEL, (p + 1) * PANEL)
 
-    low, high = rhs_sum.total()
-    out_ref[0:width // 2] = jnp.dot(low, inv[...], precision=lax.Precision.HIGHEST, preferred_element_type=jnp.float32)
-    out_ref[width // 2:] = jnp.dot(high, inv[...], precision=lax.Precision.HIGHEST, preferred_element_type=jnp.float32)
+    for part_of, total in enumerate(rhs_sum.total()):
+        at = slice(part_of * (width // 2), (part_of + 1) * (width // 2))
+        first = exact_dot(total, inv[...])
+        out_ref[at] = first + exact_dot(total - exact_dot(first, whole_gram[...]), inv[...])
 
     gram_sum.finish()
     rhs_sum.finish()
@@ -379,6 +422,7 @@
             pltpu.VMEM((NX, width, rank), jnp.float32),
             pltpu.VMEM((6, width // 2, rank), jnp.float32),
             pltpu.VMEM((rank, rank), jnp.float32),
+            pltpu.VMEM((rank, rank), jnp.float32),
             pltpu.SemaphoreType.DMA((edges,)),
             pltpu.SemaphoreType.DMA((edges,)),
             pltpu.SemaphoreType.DMA((2,)),

time: 118 us -> 107 us (0.907)
  Pallas kernels: 114 us -> 104 us
    pallas_call x1, Pallas kernels: 114 us -> 104 us  [solved_row(): pl.pallas_call(kernel, out_shape=jax.ShapeDtypeStruct((width, rank), jnp....]
where the time goes in v3:
time: 107 us
  Pallas kernels  104 us (97%)
  local copies, waits for them, and re-layouts  1.87 us (2%)
  other arithmetic  1.29 us (1%)
    pallas_call x1, Pallas kernels, solved_row(): pl.pallas_call(kernel, out_shape=jax.ShapeDtypeStruct((width, rank), jnp....  104 us

profile of v3, /device:TPU:1, one launch (start us, length us, event | category | flops | bytes accessed | tf_op | source)
XLA Modules:
  0.0 107.3 jit_solution(8740501727925938551)
XLA Ops:
  0.0 0.8 convert_reduce_fusion
  0.8 0.5 fusion.firsts
  1.3 104.1 %solve_rows.1 = f32[512,256]{1,0:T(8,128)} custom-call(bf16[8192,512]{1,0:T(8,128)(2,1)} %bitcast.5, s32[8]{0:T(128)} %fusion.firsts, s32[128]{0:T(128)} %bitcast.9, s32[128]{0:T(128)} %bitcast.10, bf16[32,16,256]{2,1,0:T(8,128)(2,1)} %bitcast.7), custom_call_target="tpu_custom_call" | custom-call | tf_op jit(solution)/shard_map/solve_rows/pallas_call | solution.py:400
  105.4 1.9 %copy.6 = f32[1,512,256]{2,1,0:T(8,128)} copy(f32[1,512,256]{2,1,0:T(8,128)} %bitcast.6) | data formatting | bytes 1048576

commit v4 on v3

--- a/solution.py
+++ b/solution.py
@@ -50,25 +50,32 @@
     return sorted(children(piece, *node), key=lambda kid: -depth(piece, kid))
 
 
-def order_of_arrival(lat=1.0, rate=0.164):
+def order_of_arrival(late=20.0, lat=1.0, rate=0.082):
     free, heap, count = {}, [], 0
 
-    def send(now, piece, par, kid):
+    def send(now, half, piece, par, kid):
         link = (kid[0] - par[0], kid[1] - par[1])
         free[link] = max(now, free.get(link, 0.0)) + PIECES[piece][6] * rate
-        heapq.heappush(heap, (free[link] + lat, count, piece, kid))
+        heapq.heappush(heap, (free[link] + lat, count, (half, piece, kid)))
 
     own = [(piece, kid) for piece in range(len(PIECES)) for kid in children(piece, 0, 0)]
     own.sort(key=lambda edge: -depth(*edge))
     for piece, kid in own:
-        send(0.0, piece, (0, 0), kid)
+        send(0.0, 0, piece, (0, 0), kid)
         count += 1
+    heapq.heappush(heap, (late, count, None))
+    count += 1
     order = []
     while heap:
-        now, _, piece, node = heapq.heappop(heap)
-        order.append((piece, node))
-        for kid in by_depth(piece, node):
-            send(now, piece, node, kid)
+        now, _, what = heapq.heappop(heap)
+        order.append(what)
+        if what is None:
+            todo = [(1, piece, (0, 0), kid) for piece, kid in own]
+        else:
+            half, piece, node = what
+            todo = [(half, piece, node, kid) for kid in by_depth(piece, node)]
+        for one in todo:
+            send(now, *one)
             count += 1
     return own, order
 
@@ -220,35 +227,41 @@
 
 
 def kernel(
-    obs_hbm, firsts, rows_s, cols_s, fac_hbm, out_ref, fall, obs_v, obs_t, fac_t, win, eye,
-    gram, gram_near, gram_ring, rhs, rhs_near, rhs_ring, inv, whole_gram, send_sem, recv_sem, loc_sem, sum_send, sum_recv
+    obs_hbm, firsts, rows_s, cols_s, fac_hbm, out_ref, fall0, fall1, obs_v, sel0, sel1, turn0, turn1, masked, eye,
+    gram0, gram0_near, gram0_ring, gram1, gram1_near, gram1_ring, rhs0, rhs0_near, rhs0_ring, rhs1, rhs1_near, rhs1_ring,
+    rhs_all, inv, whole_gram, send_sem, recv_sem, loc_sem, sum_send, sum_recv
 ):
     wide = lax.axis_index("wide")
     narrow = lax.axis_index("narrow")
     my_y, my_z = wide // NZ, wide % NZ
+    my_x, my_core = narrow // 2, narrow % 2
     own, order = order_of_arrival()
-    number = {edge: at for at, edge in enumerate(order)}
+    number = {what: at for at, what in enumerate(order)}
     shard = fac_hbm.shape[0]
     slots = cols_s.shape[0]
-    part = obs_hbm.shape[0] // slots
-    width = obs_hbm.shape[1]
     rank = fac_hbm.shape[2]
+    half = rank // 2
+    lanes, width = obs_v.shape[1:]
+    part = lanes // 2
     groups = part // GROUP
-    nothing = (fall.shape[0] - groups) // groups
-    lanes = 2 * part
+    falls, sels, turns = (fall0, fall1), (sel0, sel1), (turn0, turn1)
 
     def device(dy, dz):
         return (((my_y + dy + NY) % NY) * NZ + (my_z + dz + NZ) % NZ, narrow)
-
-    my_x, my_core = narrow // 2, narrow % 2
 
     def beside(dx, other):
         core = 1 - my_core if other else my_core
         return (wide, (my_x + dx + NX) % NX * 2 + core)
 
-    fac_copy = pltpu.make_async_copy(fac_hbm, fall.at[pl.ds(wide * shard, shard)], loc_sem.at[0])
-    fac_copy.start()
-    obs_copy = pltpu.make_async_copy(obs_hbm, obs_v, loc_sem.at[1])
+    fac_copies = [
+        pltpu.make_async_copy(
+            fac_hbm.at[:, :, h * half:(h + 1) * half], falls[h].at[pl.ds(wide * shard, shard)], loc_sem.at[h]
+        )
+        for h in range(2)
+    ]
+    for one in fac_copies:
+        one.start()
+    obs_copy = pltpu.make_async_copy(obs_hbm, obs_v, loc_sem.at[2])
     obs_copy.start()
 
     barrier = pltpu.get_barrier_semaphore()
@@ -256,16 +269,14 @@
     partners += [beside(0, 1), beside(1, 0), beside(-1, 0)]
     for partner in partners:
         pl.semaphore_signal(barrier, inc=1, device_id=partner, device_id_type=MESH)
-    fac_copy.wait()
+    for one in fac_copies:
+        one.wait()
     pl.semaphore_wait(barrier, len(partners))
 
-    def place_of(piece, node):
+    def copy(h, piece, node, to, step):
+        at = number[(h, piece, to)]
         source = ((my_y - node[0] + NY) % NY) * NZ + (my_z - node[1] + NZ) % NZ
-        return fall.at[pl.ds(source * shard + PIECES[piece][5], PIECES[piece][6])]
-
-    def copy(piece, node, to, step):
-        at = number[(piece, to)]
-        place = place_of(piece, node)
+        place = falls[h].at[pl.ds(source * shard + PIECES[piece][5], PIECES[piece][6])]
         return pltpu.make_async_remote_copy(
             src_ref=place,
             dst_ref=place,
@@ -277,118 +288,161 @@
 
     sent = []
 
-    def pass_on(piece, node, kid):
-        sent.append(copy(piece, node, kid, (kid[0] - node[0], kid[1] - node[1])))
+    def pass_on(h, piece, node, kid):
+        sent.append(copy(h, piece, node, kid, (kid[0] - node[0], kid[1] - node[1])))
         sent[-1].start()
 
     for piece, kid in own:
-        pass_on(piece, (0, 0), kid)
+        pass_on(0, piece, (0, 0), kid)
 
     down = lax.broadcasted_iota(jnp.int32, (rank, rank), 0)
     across = lax.broadcasted_iota(jnp.int32, (rank, rank), 1)
-    eye[...] = jnp.where(down == across, 1.0, 0.0).astype(jnp.bfloat16)
-    for t in range(groups):
-        fall[nothing * groups + t] = jnp.zeros((GROUP, rank), jnp.bfloat16)
-
-    def turned(tile):
-        flat = lax.dot_general(eye[...], tile, (((1,), (1,)), ((), ())), preferred_element_type=jnp.float32)
-        return flat.astype(jnp.bfloat16)
-
-    def block(col):
-        return jnp.concatenate([fall[col * groups + t] for t in range(groups)], axis=0)
-
+    lane = lax.broadcasted_iota(jnp.int32, (1, lanes), 1)
+    eye[...] = jnp.where(down == across, 1.0, 0.0)[:half, :half].astype(jnp.bfloat16)
     obs_copy.wait()
+
+    gram_sums = [
+        RowSum(gram0, gram0_near, gram0_ring, sum_send, sum_recv, 0, my_x, my_core, beside),
+        RowSum(gram1, gram1_near, gram1_ring, sum_send, sum_recv, 10, my_x, my_core, beside),
+    ]
+    rhs_sums = [
+        RowSum(rhs0, rhs0_near, rhs0_ring, sum_send, sum_recv, 20, my_x, my_core, beside),
+        RowSum(rhs1, rhs1_near, rhs1_ring, sum_send, sum_recv, 30, my_x, my_core, beside),
+    ]
+
+    def select(h, step):
+        for t in range(2):
+            pair = step * 2 + t
+            tile = jnp.concatenate(
+                [falls[h][cols_s[pair * 2 + k] * groups + g] for k in range(2) for g in range(groups)], axis=0
+            )
+            sels[h][pair] = tile
+            flat = lax.dot_general(eye[...], tile, (((1,), (1,)), ((), ())), preferred_element_type=jnp.float32)
+            turns[h][pair] = flat.astype(jnp.bfloat16)
+
+    pairs = WINDOW // 2
+
+    def mask(h, row):
+        first = firsts[row]
+        for t in range(pairs):
+            keep = [jnp.where(rows_s[(first + t) * 2 + k] == row, 1.0, 0.0) for k in range(2)]
+            keep = jnp.where(lane < part, keep[0], keep[1]).astype(jnp.bfloat16)
+            masked[:, t * lanes:(t + 1) * lanes] = turns[h][first + t] * keep
+
+    def product(first, load):
+        total = None
+        for t in range(0, pairs, 2):
+            both = [load(first + k) for k in range(t, min(t + 2, pairs))]
+            left = masked[:, t * lanes:(t + len(both)) * lanes]
+            right = both[0] if len(both) == 1 else jnp.concatenate(both, axis=0)
+            one = jnp.dot(left, right, preferred_element_type=jnp.float32)
+            total = one if total is None else total + one
+        return total
+
+    def gram_of(h, row):
+        if h == 0:
+            gram0[row] = product(firsts[row], lambda at: sel0[at])
+        else:
+            gram1[row] = product(firsts[row], lambda at: jnp.concatenate([sel0[at], sel1[at]], axis=1))
+
+    def rhs_of(h, row, tile):
+        at = slice(tile * rank, (tile + 1) * rank)
+        (rhs0, rhs1)[h][row, :, at] = product(firsts[row], lambda pair: obs_v[pair, :, at])
+
+    def row_of(q, other):
+        return gram_sums[0].row((2 - q + NX) % NX, other)
+
+    def near(sums, q):
+        sums.near((2 - q + NX) % NX, q).start()
+
     wide_tiles = width // rank
-    tiles = (slots * part // rank) * wide_tiles
-    chunks = rank // lanes
-
-    def turn_obs(tile):
-        down_at, across_at = tile // wide_tiles, tile % wide_tiles
-        flat = turned(obs_v[down_at * rank:(down_at + 1) * rank, across_at * rank:(across_at + 1) * rank])
-        for t in range(chunks):
-            obs_t[down_at * chunks + t, across_at * rank:(across_at + 1) * rank] = flat[:, t * lanes:(t + 1) * lanes]
-
+    steps = slots // 4
+    jobs = []
+    for step in range(0, steps, 2):
+        jobs.append(lambda step=step: (select(0, step), select(0, step + 1)))
+    for q in range(NX):
+        for other in (True, False):
+            jobs.append(lambda q=q, other=other: (mask(0, row_of(q, other)), gram_of(0, row_of(q, other))))
+            if other:
+                jobs[-1] = lambda q=q: (mask(0, row_of(q, True)), gram_of(0, row_of(q, True)), near(gram_sums[0], q))
+            for tile in range(wide_tiles):
+                jobs.append(lambda q=q, other=other, tile=tile: rhs_of(0, row_of(q, other), tile))
+        jobs.append(lambda q=q: rhs_sums[0].near((2 - q + NX) % NX, q).start())
+    for q in range(NX):
+        jobs.append(lambda q=q: gram_sums[0].fold(q))
+    for q in range(NX):
+        jobs.append(lambda q=q: rhs_sums[0].fold(q))
+    jobs.append(gram_sums[0].forward)
+    jobs.append(rhs_sums[0].forward)
+
+    ready = max(at for at, what in enumerate(order) if what is not None and what[0] == 0)
     done = 0
-    for at, (piece, node) in enumerate(order):
-        copy(piece, node, node, (1, 0)).wait_recv()
+    for at, what in enumerate(order):
+        if what is None:
+            for piece, kid in own:
+                pass_on(1, piece, (0, 0), kid)
+            continue
+        h, piece, node = what
+        copy(h, piece, node, node, (1, 0)).wait_recv()
         for kid in by_depth(piece, node):
-            pass_on(piece, node, kid)
-        while done < tiles and done * 100 < (at + 1) * tiles:
-            turn_obs(done)
+            pass_on(h, piece, node, kid)
+        while done < len(jobs) and at >= ready and done * (len(order) - 1 - ready) <= (at - ready) * len(jobs):
+            jobs[done]()
             done += 1
-
-    @pl.loop(0, slots * part // rank)
-    def turn_factors(step):
-        few = rank // part
-        flat = turned(jnp.concatenate([block(cols_s[step * few + t]) for t in range(few)], axis=0))
-        for t in range(chunks):
-            fac_t[step * chunks + t] = flat[:, t * lanes:(t + 1) * lanes]
-
-    def window_of(ref, i):
-        first = firsts[i]
-        return jnp.concatenate([ref[first + t] for t in range(WINDOW // 2)], axis=1)
-
-    gram_sum = RowSum(gram, gram_near, gram_ring, sum_send, sum_recv, 0, my_x, my_core, beside)
-    rhs_sum = RowSum(rhs, rhs_near, rhs_ring, sum_send, sum_recv, 10, my_x, my_core, beside)
-    half = rank // 2
-
-    def gram_of(row):
-        first = firsts[row] * 2
-        for t in range(WINDOW):
-            col = jnp.where(rows_s[first + t] == row, cols_s[first + t], nothing)
-            win[row, t * part:(t + 1) * part, :] = block(col)
-        whole = jnp.dot(window_of(fac_t, row), win[row], preferred_element_type=jnp.float32)
-        gram[row, 0:rank, :] = whole[:, :half]
-        gram[row, rank:rank + half, :] = whole[half:, half:]
-
-    def rhs_of(row):
-        rhs[row] = jnp.dot(window_of(obs_t, row), win[row], preferred_element_type=jnp.float32)
+    while done < len(jobs):
+        jobs[done]()
+        done += 1
+
+    pl.loop(0, steps)(functools.partial(select, 1))
 
     @pl.loop(0, NX)
     def grams(q):
-        ahead = (2 - q + NX) % NX
-        gram_of(gram_sum.row(ahead, True))
-        gram_sum.near(ahead, q).start()
-        gram_of(gram_sum.row(ahead, False))
+        for other in (True, False):
+            mask(1, row_of(q, other))
+            gram_of(1, row_of(q, other))
+            if other:
+                near(gram_sums[1], q)
 
     def rhs_pair(q):
-        ahead = (2 - q + NX) % NX
-        rhs_of(rhs_sum.row(ahead, True))
-        rhs_sum.near(ahead, q).start()
-        rhs_of(rhs_sum.row(ahead, False))
+        for other in (True, False):
+            mask(1, row_of(q, other))
+            for tile in range(wide_tiles):
+                rhs_of(1, row_of(q, other), tile)
+            if other:
+                near(rhs_sums[1], q)
 
     for q in range(NX):
-        gram_sum.fold(q)
+        gram_sums[1].fold(q)
     pl.loop(0, 2)(rhs_pair)
-    gram_sum.forward()
-    rhs_sum.fold(0)
-    rhs_sum.fold(1)
+    gram_sums[1].forward()
+    rhs_sums[1].fold(0)
+    rhs_sums[1].fold(1)
     pl.loop(2, NX)(rhs_pair)
-    rhs_sum.fold(2)
-    rhs_sum.fold(3)
-
-    low, high = gram_sum.total()
-    packed = jnp.concatenate([low, high], axis=0)
+    rhs_sums[1].fold(2)
+    rhs_sums[1].fold(3)
+
+    rhs_all[:, :half] = jnp.concatenate(rhs_sums[0].total(), axis=0).T
     same = jnp.where(down == across, LAMBDA_REG, 0.0)
-    inv[:half, :half] = packed[:half] + same[:half, :half]
-    inv[half:, :half] = packed[half:rank]
-    inv[:half, half:] = packed[half:rank].T
-    inv[half:, half:] = packed[rank:] + same[:half, :half]
-
+    upper = jnp.concatenate(gram_sums[0].total(), axis=0)
+    lower = jnp.concatenate(gram_sums[1].total(), axis=0)
+    inv[:half, :half] = upper + same[:half, :half]
+    inv[half:, :] = lower + same[half:, :]
+    inv[:half, half:] = lower[:, :half].T
     whole_gram[...] = inv[...]
-    panels = rank // PANEL
-    for p in range(panels):
-        if p == panels // 2:
-            rhs_sum.forward()
+    for p in range(rank // PANEL):
+        if p == 1:
+            rhs_sums[1].forward()
         eliminate(inv, p * PANEL, (p + 1) * PANEL)
 
-    for part_of, total in enumerate(rhs_sum.total()):
-        at = slice(part_of * (width // 2), (part_of + 1) * (width // 2))
+    rhs_all[:, half:] = jnp.concatenate(rhs_sums[1].total(), axis=0).T
+    for tile in range(wide_tiles):
+        at = slice(tile * rank, (tile + 1) * rank)
+        total = rhs_all[at]
         first = exact_dot(total, inv[...])
         out_ref[at] = first + exact_dot(total - exact_dot(first, whole_gram[...]), inv[...])
 
-    gram_sum.finish()
-    rhs_sum.finish()
+    for sums in gram_sums + rhs_sums:
+        sums.finish()
     for out in sent:
         out.wait_send()
 
@@ -396,7 +450,17 @@
 def solved_row(obs, rows, cols, factors):
     slots, part, width = obs.shape
     rank = factors.shape[-1]
+    half = rank // 2
     edges = len(order_of_arrival()[1])
+    every = NY * NZ * RW * part // GROUP
+
+    def sums(rows, cols):
+        return [
+            pltpu.VMEM((RW, rows, cols), jnp.float32),
+            pltpu.VMEM((NX, rows, cols), jnp.float32),
+            pltpu.VMEM((6, rows // 2, cols), jnp.float32),
+        ]
+
     return pl.pallas_call(
         kernel,
         out_shape=jax.ShapeDtypeStruct((width, rank), jnp.float32),
@@ -409,30 +473,32 @@
         ],
         out_specs=pl.BlockSpec(memory_space=pltpu.VMEM),
         scratch_shapes=[
-            pltpu.VMEM(((NY * NZ * RW + 1) * part // GROUP, GROUP, rank), jnp.bfloat16),
-            pltpu.VMEM((slots * part, width), jnp.bfloat16),
-            pltpu.VMEM((slots // 2, width, 2 * part), jnp.bfloat16),
-            pltpu.VMEM((slots // 2, rank, 2 * part), jnp.bfloat16),
-            pltpu.VMEM((RW, WINDOW * part, rank), jnp.bfloat16),
-            pltpu.VMEM((rank, rank), jnp.bfloat16),
-            pltpu.VMEM((RW, rank + rank // 2, rank // 2), jnp.float32),
-            pltpu.VMEM((NX, rank + rank // 2, rank // 2), jnp.float32),
-            pltpu.VMEM((6, (rank + rank // 2) // 2, rank // 2), jnp.float32),
-            pltpu.VMEM((RW, width, rank), jnp.float32),
-            pltpu.VMEM((NX, width, rank), jnp.float32),
-            pltpu.VMEM((6, width // 2, rank), jnp.float32),
+            pltpu.VMEM((every, GROUP, half), jnp.bfloat16),
+            pltpu.VMEM((every, GROUP, half), jnp.bfloat16),
+            pltpu.VMEM((slots // 2, 2 * part, width), jnp.bfloat16),
+            pltpu.VMEM((slots // 2, 2 * part, half), jnp.bfloat16),
+            pltpu.VMEM((slots // 2, 2 * part, half), jnp.bfloat16),
+            pltpu.VMEM((slots // 2, half, 2 * part), jnp.bfloat16),
+            pltpu.VMEM((slots // 2, half, 2 * part), jnp.bfloat16),
+            pltpu.VMEM((half, WINDOW * part), jnp.bfloat16),
+            pltpu.VMEM((half, half), jnp.bfloat16),
+            *sums(half, half),
+            *sums(half, rank),
+            *sums(half, width),
+            *sums(half, width),
+            pltpu.VMEM((width, rank), jnp.float32),
             pltpu.VMEM((rank, rank), jnp.float32),
             pltpu.VMEM((rank, rank), jnp.float32),
             pltpu.SemaphoreType.DMA((edges,)),
             pltpu.SemaphoreType.DMA((edges,)),
-            pltpu.SemaphoreType.DMA((2,)),
-            pltpu.SemaphoreType.DMA((20,)),
-            pltpu.SemaphoreType.DMA((20,)),
+            pltpu.SemaphoreType.DMA((3,)),
+            pltpu.SemaphoreType.DMA((40,)),
+            pltpu.SemaphoreType.DMA((40,)),
         ],
         compiler_params=pltpu.CompilerParams(collective_id=0, has_side_effects=True, vmem_limit_bytes=60 * 1024 * 1024),
         name="solve_rows",
     )(
-        obs.reshape(slots * part, width),
+        obs.reshape(slots // 2, 2 * part, width),
         window_starts(rows),
         rows,
         cols,

time: 107 us -> 110 us (1.028)
  Pallas kernels: 104 us -> 107 us
    pallas_call x1, Pallas kernels: 104 us -> 107 us  [solved_row(): pl.pallas_call(kernel, out_shape=jax.ShapeDtypeStruct((width, rank), jnp....]
where the time goes in v4:
time: 110 us
  Pallas kernels  107 us (97%)
  local copies, waits for them, and re-layouts  1.87 us (2%)
  other arithmetic  1.29 us (1%)
    pallas_call x1, Pallas kernels, solved_row(): pl.pallas_call(kernel, out_shape=jax.ShapeDtypeStruct((width, rank), jnp....  107 us

profile of v4, /device:TPU:1, one launch (start us, length us, event | category | flops | bytes accessed | tf_op | source)
XLA Modules:
  0.0 109.9 jit_solution(17062179493672696080)
XLA Ops:
  0.0 0.8 convert_reduce_fusion
  0.8 0.5 fusion.firsts
  1.3 106.7 %solve_rows.1 = f32[512,256]{1,0:T(8,128)} custom-call(bf16[64,128,512]{2,1,0:T(8,128)(2,1)} %bitcast.5, s32[8]{0:T(128)} %fusion.firsts, s32[128]{0:T(128)} %bitcast.9, s32[128]{0:T(128)} %bitcast.10, bf16[32,16,256]{2,1,0:T(8,128)(2,1)} %bitcast.7), custom_call_target="tpu_custom_call" | custom-call | tf_op jit(solution)/shard_map/solve_rows/pallas_call | solution.py:464
  108.0 1.9 %copy.6 = f32[1,512,256]{2,1,0:T(8,128)} copy(f32[1,512,256]{2,1,0:T(8,128)} %bitcast.6) | data formatting | bytes 1048576

commit v5 on v4

--- a/solution.py
+++ b/solution.py
@@ -23,6 +23,7 @@
 )
 GROUP = 16
 PANEL = 64
+AT_ONCE = 8
 
 
 def children(piece, dy, dz):
@@ -191,22 +192,40 @@
     down = lax.broadcasted_iota(jnp.int32, (size, size), 0)
     across = lax.broadcasted_iota(jnp.int32, (size, size), 1)
     lane = across[0:8]
+
+    def spread(values, j):
+        return [jnp.broadcast_to(values[:, j + k:j + k + 1], (size, size)) for k in range(4)]
+
+    def tall(row):
+        return jnp.concatenate([row] * (size // 8), axis=0)
+
+    def mix(weights, rows):
+        return (weights[0] * rows[0] + weights[1] * rows[1]) + (weights[2] * rows[2] + weights[3] * rows[3])
+
+    cols = spread(block, 0)
     for j in range(0, size, 4):
-        cols = [jnp.broadcast_to(block[:, j + k:j + k + 1], (size, size)) for k in range(4)]
-        rows = [jnp.broadcast_to(block[j + k:j + k + 1], (8, size)) for k in range(4)]
+        later = spread(block, j + 4) if j + 4 < size else []
         pivot = [[jnp.broadcast_to(cols[max(k, l)][j + min(k, l):j + min(k, l) + 1], (8, size)) for l in range(4)] for k in range(4)]
         inverse = inverse_4x4(pivot)
-        rest = jnp.where((across >= j) & (across < j + 4), 0.0, block)
+        ahead = []
+        for old in later:
+            here = [jnp.broadcast_to(old[j + k:j + k + 1], (8, size)) for k in range(4)]
+            new_rows = [tall(mix(inverse[k], here)) for k in range(4)]
+            new = old - mix(cols, new_rows)
+            for k in range(4):
+                new = jnp.where(down == j + k, new_rows[k], new)
+            ahead.append(new)
+        rows = [jnp.broadcast_to(block[j + k:j + k + 1], (8, size)) for k in range(4)]
         done = []
         for k in range(4):
-            row = (inverse[k][0] * rows[0] + inverse[k][1] * rows[1]) + (inverse[k][2] * rows[2] + inverse[k][3] * rows[3])
+            row = mix(inverse[k], rows)
             for l in range(4):
                 row = jnp.where(lane == j + l, inverse[k][l], row)
-            done.append(jnp.concatenate([row] * (size // 8), axis=0))
-        rest = rest - ((cols[0] * done[0] + cols[1] * done[1]) + (cols[2] * done[2] + cols[3] * done[3]))
+            done.append(tall(row))
+        block = jnp.where((across >= j) & (across < j + 4), 0.0, block) - mix(cols, done)
         for k in range(4):
-            rest = jnp.where(down == j + k, done[k], rest)
-        block = rest
+            block = jnp.where(down == j + k, done[k], block)
+        cols = ahead
     return block
 
 
@@ -227,7 +246,7 @@
 
 
 def kernel(
-    obs_hbm, firsts, rows_s, cols_s, fac_hbm, out_ref, fall0, fall1, obs_v, sel0, sel1, turn0, turn1, masked, eye,
+    obs_hbm, firsts, rows_s, cols_s, fac_hbm, out_ref, fall0, fall1, obs_v, sel0, sel1, turn0, turn1, keeps, masked, eye,
     gram0, gram0_near, gram0_ring, gram1, gram1_near, gram1_ring, rhs0, rhs0_near, rhs0_ring, rhs1, rhs1_near, rhs1_ring,
     rhs_all, inv, whole_gram, send_sem, recv_sem, loc_sem, sum_send, sum_recv
 ):
@@ -297,7 +316,7 @@
 
     down = lax.broadcasted_iota(jnp.int32, (rank, rank), 0)
     across = lax.broadcasted_iota(jnp.int32, (rank, rank), 1)
-    lane = lax.broadcasted_iota(jnp.int32, (1, lanes), 1)
+    lane = lax.broadcasted_iota(jnp.int32, (GROUP, lanes), 1)
     eye[...] = jnp.where(down == across, 1.0, 0.0)[:half, :half].astype(jnp.bfloat16)
     obs_copy.wait()
 
@@ -311,8 +330,8 @@
     ]
 
     def select(h, step):
-        for t in range(2):
-            pair = step * 2 + t
+        for t in range(AT_ONCE):
+            pair = step * AT_ONCE + t
             tile = jnp.concatenate(
                 [falls[h][cols_s[pair * 2 + k] * groups + g] for k in range(2) for g in range(groups)], axis=0
             )
@@ -322,18 +341,23 @@
 
     pairs = WINDOW // 2
 
+    def keep_of(row):
+        first = firsts[row]
+        for t in range(pairs):
+            keep = [jnp.where(rows_s[(first + t) * 2 + k] == row, 1.0, 0.0) for k in range(2)]
+            keeps[row, t] = jnp.where(lane < part, keep[0], keep[1]).astype(jnp.bfloat16)
+
     def mask(h, row):
         first = firsts[row]
         for t in range(pairs):
-            keep = [jnp.where(rows_s[(first + t) * 2 + k] == row, 1.0, 0.0) for k in range(2)]
-            keep = jnp.where(lane < part, keep[0], keep[1]).astype(jnp.bfloat16)
-            masked[:, t * lanes:(t + 1) * lanes] = turns[h][first + t] * keep
-
-    def product(first, load):
-        total = None
+            keep = jnp.concatenate([keeps[row, t]] * (half // GROUP), axis=0)
+            masked[row, :, t * lanes:(t + 1) * lanes] = turns[h][first + t] * keep
+
+    def product(row, load):
+        first, total = firsts[row], None
         for t in range(0, pairs, 2):
             both = [load(first + k) for k in range(t, min(t + 2, pairs))]
-            left = masked[:, t * lanes:(t + len(both)) * lanes]
+            left = masked[row, :, t * lanes:(t + len(both)) * lanes]
             right = both[0] if len(both) == 1 else jnp.concatenate(both, axis=0)
             one = jnp.dot(left, right, preferred_element_type=jnp.float32)
             total = one if total is None else total + one
@@ -341,13 +365,13 @@
 
     def gram_of(h, row):
         if h == 0:
-            gram0[row] = product(firsts[row], lambda at: sel0[at])
+            gram0[row] = product(row, lambda at: sel0[at])
         else:
-            gram1[row] = product(firsts[row], lambda at: jnp.concatenate([sel0[at], sel1[at]], axis=1))
+            gram1[row] = product(row, lambda at: jnp.concatenate([sel0[at], sel1[at]], axis=1))
 
     def rhs_of(h, row, tile):
         at = slice(tile * rank, (tile + 1) * rank)
-        (rhs0, rhs1)[h][row, :, at] = product(firsts[row], lambda pair: obs_v[pair, :, at])
+        (rhs0, rhs1)[h][row, :, at] = product(row, lambda pair: obs_v[pair, :, at])
 
     def row_of(q, other):
         return gram_sums[0].row((2 - q + NX) % NX, other)
@@ -356,10 +380,10 @@
         sums.near((2 - q + NX) % NX, q).start()
 
     wide_tiles = width // rank
-    steps = slots // 4
+    steps = slots // 2 // AT_ONCE
     jobs = []
-    for step in range(0, steps, 2):
-        jobs.append(lambda step=step: (select(0, step), select(0, step + 1)))
+    for step in range(steps):
+        jobs.append(lambda step=step: select(0, step))
     for q in range(NX):
         for other in (True, False):
             jobs.append(lambda q=q, other=other: (mask(0, row_of(q, other)), gram_of(0, row_of(q, other))))
@@ -375,6 +399,7 @@
     jobs.append(gram_sums[0].forward)
     jobs.append(rhs_sums[0].forward)
 
+    pl.loop(0, RW)(keep_of)
     ready = max(at for at, what in enumerate(order) if what is not None and what[0] == 0)
     done = 0
     for at, what in enumerate(order):
@@ -405,7 +430,6 @@
 
     def rhs_pair(q):
         for other in (True, False):
-            mask(1, row_of(q, other))
             for tile in range(wide_tiles):
                 rhs_of(1, row_of(q, other), tile)
             if other:
@@ -480,7 +504,8 @@
             pltpu.VMEM((slots // 2, 2 * part, half), jnp.bfloat16),
             pltpu.VMEM((slots // 2, half, 2 * part), jnp.bfloat16),
             pltpu.VMEM((slots // 2, half, 2 * part), jnp.bfloat16),
-            pltpu.VMEM((half, WINDOW * part), jnp.bfloat16),
+            pltpu.VMEM((RW, WINDOW // 2, GROUP, 2 * part), jnp.bfloat16),
+            pltpu.VMEM((RW, half, WINDOW * part), jnp.bfloat16),
             pltpu.VMEM((half, half), jnp.bfloat16),
             *sums(half, half),
             *sums(half, rank),

time: 110 us -> 102 us (0.927)
  Pallas kernels: 107 us -> 99 us
    pallas_call x1, Pallas kernels: 107 us -> 99 us  [solved_row(): pl.pallas_call(kernel, out_shape=jax.ShapeDtypeStruct((width, rank), jnp....]
where the time goes in v5:
time: 102 us
  Pallas kernels  99 us (97%)
  local copies, waits for them, and re-layouts  1.87 us (2%)
  other arithmetic  1.29 us (1%)
    pallas_call x1, Pallas kernels, solved_row(): pl.pallas_call(kernel, out_shape=jax.ShapeDtypeStruct((width, rank), jnp....  99 us

profile of v5, /device:TPU:1, one launch (start us, length us, event | category | flops | bytes accessed | tf_op | source)
XLA Modules:
  0.0 102.2 jit_solution(11536986326216271855)
XLA Ops:
  0.0 0.8 convert_reduce_fusion
  0.8 0.5 fusion.firsts
  1.3 99.0 %solve_rows.1 = f32[512,256]{1,0:T(8,128)} custom-call(bf16[64,128,512]{2,1,0:T(8,128)(2,1)} %bitcast.5, s32[8]{0:T(128)} %fusion.firsts, s32[128]{0:T(128)} %bitcast.9, s32[128]{0:T(128)} %bitcast.10, bf16[32,16,256]{2,1,0:T(8,128)(2,1)} %bitcast.7), custom_call_target="tpu_custom_call" | custom-call | tf_op jit(solution)/shard_map/solve_rows/pallas_call | solution.py:488
  100.3 1.9 %copy.6 = f32[1,512,256]{2,1,0:T(8,128)} copy(f32[1,512,256]{2,1,0:T(8,128)} %bitcast.6) | data formatting | bytes 1048576

commit v6 on v5

--- a/solution.py
+++ b/solution.py
@@ -187,8 +187,9 @@
     ]
 
 
-def small_inverse(block):
+def small_inverse(block, begin=0, end=None):
     size = block.shape[0]
+    end = size if end is None else end
     down = lax.broadcasted_iota(jnp.int32, (size, size), 0)
     across = lax.broadcasted_iota(jnp.int32, (size, size), 1)
     lane = across[0:8]
@@ -202,9 +203,9 @@
     def mix(weights, rows):
         return (weights[0] * rows[0] + weights[1] * rows[1]) + (weights[2] * rows[2] + weights[3] * rows[3])
 
-    cols = spread(block, 0)
-    for j in range(0, size, 4):
-        later = spread(block, j + 4) if j + 4 < size else []
+    cols = spread(block, begin)
+    for j in range(begin, end, 4):
+        later = spread(block, j + 4) if j + 4 < end else []
         pivot = [[jnp.broadcast_to(cols[max(k, l)][j + min(k, l):j + min(k, l) + 1], (8, size)) for l in range(4)] for k in range(4)]
         inverse = inverse_4x4(pivot)
         ahead = []
@@ -233,8 +234,9 @@
     return jnp.dot(x, y, precision=lax.Precision.HIGHEST, preferred_element_type=jnp.float32)
 
 
-def eliminate(inv, low, high):
-    pivot = small_inverse(inv[low:high, low:high])
+def eliminate(inv, low, high, pivot=None):
+    if pivot is None:
+        pivot = small_inverse(inv[low:high, low:high])
     inv[low:high, :] = exact_dot(pivot, inv[low:high, :])
     inv[low:high, low:high] = pivot
     rows = inv[low:high, :]
@@ -246,9 +248,9 @@
 
 
 def kernel(
-    obs_hbm, firsts, rows_s, cols_s, fac_hbm, out_ref, fall0, fall1, obs_v, sel0, sel1, turn0, turn1, keeps, masked, eye,
+    obs_hbm, firsts, rows_s, cols_s, fac_hbm, out_ref, more_ref, fall0, fall1, obs_v, sel0, sel1, turn0, turn1, keeps, masked, eye,
     gram0, gram0_near, gram0_ring, gram1, gram1_near, gram1_ring, rhs0, rhs0_near, rhs0_ring, rhs1, rhs1_near, rhs1_ring,
-    rhs_all, inv, whole_gram, send_sem, recv_sem, loc_sem, sum_send, sum_recv
+    rhs_all, inv, whole_gram, corner, small, send_sem, recv_sem, loc_sem, sum_send, sum_recv
 ):
     wide = lax.axis_index("wide")
     narrow = lax.axis_index("narrow")
@@ -384,20 +386,44 @@
     jobs = []
     for step in range(steps):
         jobs.append(lambda step=step: select(0, step))
-    for q in range(NX):
-        for other in (True, False):
-            jobs.append(lambda q=q, other=other: (mask(0, row_of(q, other)), gram_of(0, row_of(q, other))))
-            if other:
-                jobs[-1] = lambda q=q: (mask(0, row_of(q, True)), gram_of(0, row_of(q, True)), near(gram_sums[0], q))
-            for tile in range(wide_tiles):
-                jobs.append(lambda q=q, other=other, tile=tile: rhs_of(0, row_of(q, other), tile))
-        jobs.append(lambda q=q: rhs_sums[0].near((2 - q + NX) % NX, q).start())
-    for q in range(NX):
-        jobs.append(lambda q=q: gram_sums[0].fold(q))
-    for q in range(NX):
-        jobs.append(lambda q=q: rhs_sums[0].fold(q))
-    jobs.append(gram_sums[0].forward)
-    jobs.append(rhs_sums[0].forward)
+    def gram_job(q, other):
+        mask(0, row_of(q, other))
+        gram_of(0, row_of(q, other))
+        if other:
+            near(gram_sums[0], q)
+
+    def rhs_job(q, other, tile):
+        rhs_of(0, row_of(q, other), tile)
+        if other and tile == wide_tiles - 1:
+            near(rhs_sums[0], q)
+
+    def start_upper():
+        upper = jnp.concatenate(gram_sums[0].total(), axis=0)
+        corner[...] = upper + jnp.where(down == across, LAMBDA_REG, 0.0)[:half, :half]
+        inv[:half, :half] = corner[...]
+
+    def stage(p, begin):
+        at = slice(p * PANEL, (p + 1) * PANEL)
+        if begin == 0:
+            small[...] = corner[at, at]
+        small[...] = small_inverse(small[...], begin, begin + 16)
+        if begin + 16 == PANEL:
+            eliminate(corner, p * PANEL, (p + 1) * PANEL, small[...])
+
+    def rhs_jobs(other, few):
+        return [functools.partial(rhs_job, q, other, tile) for q in few for tile in range(wide_tiles)]
+
+    jobs += [functools.partial(gram_job, q, other) for other in (True, False) for q in range(NX)]
+    jobs += rhs_jobs(True, range(NX))
+    jobs += [functools.partial(gram_sums[0].fold, q) for q in range(NX)]
+    jobs += rhs_jobs(False, range(2))
+    jobs += [gram_sums[0].forward]
+    jobs += rhs_jobs(False, range(2, NX))
+    jobs += [start_upper]
+    jobs += [functools.partial(stage, 0, begin) for begin in range(0, PANEL, 16)]
+    jobs += [functools.partial(rhs_sums[0].fold, q) for q in range(NX)]
+    jobs += [functools.partial(stage, 1, begin) for begin in range(0, PANEL, 16)]
+    jobs += [rhs_sums[0].forward]
 
     pl.loop(0, RW)(keep_of)
     ready = max(at for at, what in enumerate(order) if what is not None and what[0] == 0)
@@ -421,12 +447,15 @@
     pl.loop(0, steps)(functools.partial(select, 1))
 
     @pl.loop(0, NX)
-    def grams(q):
-        for other in (True, False):
-            mask(1, row_of(q, other))
-            gram_of(1, row_of(q, other))
-            if other:
-                near(gram_sums[1], q)
+    def other_grams(q):
+        mask(1, row_of(q, True))
+        gram_of(1, row_of(q, True))
+        near(gram_sums[1], q)
+
+    @pl.loop(0, NX)
+    def own_grams(q):
+        mask(1, row_of(q, False))
+        gram_of(1, row_of(q, False))
 
     def rhs_pair(q):
         for other in (True, False):
@@ -447,15 +476,13 @@
 
     rhs_all[:, :half] = jnp.concatenate(rhs_sums[0].total(), axis=0).T
     same = jnp.where(down == across, LAMBDA_REG, 0.0)
-    upper = jnp.concatenate(gram_sums[0].total(), axis=0)
     lower = jnp.concatenate(gram_sums[1].total(), axis=0)
-    inv[:half, :half] = upper + same[:half, :half]
     inv[half:, :] = lower + same[half:, :]
     inv[:half, half:] = lower[:, :half].T
     whole_gram[...] = inv[...]
-    for p in range(rank // PANEL):
-        if p == 1:
-            rhs_sums[1].forward()
+    eliminate(inv, 0, half, corner[...])
+    rhs_sums[1].forward()
+    for p in range(half // PANEL, rank // PANEL):
         eliminate(inv, p * PANEL, (p + 1) * PANEL)
 
     rhs_all[:, half:] = jnp.concatenate(rhs_sums[1].total(), axis=0).T
@@ -463,7 +490,8 @@
         at = slice(tile * rank, (tile + 1) * rank)
         total = rhs_all[at]
         first = exact_dot(total, inv[...])
-        out_ref[at] = first + exact_dot(total - exact_dot(first, whole_gram[...]), inv[...])
+        out_ref[at] = first
+        more_ref[at] = exact_dot(total - exact_dot(first, whole_gram[...]), inv[...])
 
     for sums in gram_sums + rhs_sums:
         sums.finish()
@@ -487,7 +515,7 @@
 
     return pl.pallas_call(
         kernel,
-        out_shape=jax.ShapeDtypeStruct((width, rank), jnp.float32),
+        out_shape=(jax.ShapeDtypeStruct((width, rank), jnp.float32),) * 2,
         in_specs=[
             pl.BlockSpec(memory_space=pl.ANY),
             pl.BlockSpec(memory_space=pltpu.SMEM),
@@ -495,7 +523,7 @@
             pl.BlockSpec(memory_space=pltpu.SMEM),
             pl.BlockSpec(memory_space=pl.ANY),
         ],
-        out_specs=pl.BlockSpec(memory_space=pltpu.VMEM),
+        out_specs=(pl.BlockSpec(memory_space=pltpu.VMEM),) * 2,
         scratch_shapes=[
             pltpu.VMEM((every, GROUP, half), jnp.bfloat16),
             pltpu.VMEM((every, GROUP, half), jnp.bfloat16),
@@ -514,6 +542,8 @@
             pltpu.VMEM((width, rank), jnp.float32),
             pltpu.VMEM((rank, rank), jnp.float32),
             pltpu.VMEM((rank, rank), jnp.float32),
+            pltpu.VMEM((half, half), jnp.float32),
+            pltpu.VMEM((PANEL, PANEL), jnp.float32),
             pltpu.SemaphoreType.DMA((edges,)),
             pltpu.SemaphoreType.DMA((edges,)),
             pltpu.SemaphoreType.DMA((3,)),
@@ -537,7 +567,8 @@
 
 
 def body(obs_blocks, obs_row, obs_col, factors):
-    return solved_row(obs_blocks[0], obs_row[0], obs_col[0], factors)[None]
+    product, correction = solved_row(obs_blocks[0], obs_row[0], obs_col[0], factors)
+    return (product + correction)[None]
 
 
 def solution(mesh):

time: 102 us -> 98.2 us (0.963)
  Pallas kernels: 99 us -> 94.7 us
  other arithmetic: 1.29 us -> 3.35 us
  local copies, waits for them, and re-layouts: 1.87 us -> 0 us
    pallas_call x1, Pallas kernels: 99 us -> 94.7 us  [solved_row(): pl.pallas_call(kernel, out_shape=(jax.ShapeDtypeStruct((width, rank), jnp...]
    broadcast_in_dim x0 -> x1, other arithmetic: none -> 2.06 us  [body(): return (product + correction)[None]]
    unnamed x1 -> x0, local copies, waits for them, and re-layouts: 1.87 us -> none
where the time goes in v6:
time: 98.2 us; the launch traced here: 98.1 us
  Pallas kernels  94.7 us (96%)
  other arithmetic  3.35 us (3%)
    pallas_call x1, Pallas kernels, solved_row(): pl.pallas_call(kernel, out_shape=(jax.ShapeDtypeStruct((width, rank), jnp...  94.7 us
    broadcast_in_dim x1, other arithmetic, body(): return (product + correction)[None]  2.06 us

profile of v6, /device:TPU:1, one launch (start us, length us, event | category | flops | bytes accessed | tf_op | source)
XLA Modules:
  0.0 98.1 jit_solution(5436772715413531414)
XLA Ops:
  0.0 0.8 convert_reduce_fusion
  0.8 0.5 fusion.firsts
  1.3 94.7 %solve_rows.1 = (f32[512,256]{1,0:T(8,128)}, f32[512,256]{1,0:T(8,128)}) custom-call(bf16[64,128,512]{2,1,0:T(8,128)(2,1)} %bitcast.6, s32[8]{0:T(128)} %fusion.firsts, s32[128]{0:T(128)} %bitcast.9, s32[128]{0:T(128)} %bitcast.10, bf16[32,16,256]{2,1,0:T(8,128)(2,1)} %bitcast.7), custom_call_target="tpu_custom_call" | custom-call | tf_op jit(solution)/shard_map/solve_rows/pallas_call | solution.py:516
  96.0 2.1 %add_bitcast_fusion = f32[1,512,256]{2,1,0:T(8,128)} fusion(f32[512,256]{1,0:T(8,128)} %get-tuple-element.7, f32[512,256]{1,0:T(8,128)} %get-tuple-element.8), kind=kLoop, calls=%fused_computation | loop fusion | flops 131072 | bytes 1572864 | tf_op jit(solution)/shard_map/broadcast_in_dim | solution.py:571
